TPU v7x, 32 devices: a whole 2x2x4 slice. The times are simulated.
32 devices in a mesh: dp: 16 (over z, x, core), tensor: 2 (over y).
Axes of the slice: x: 2, y: 2, z: 4, core: 2. Of those that a mesh axis runs over, the one named last changes fastest.
Arguments:
- patches: bfloat16 [192, 64, 768], P('dp'), may hold values from -6 to 6
- visible: int32 [192], P('dp'), may hold values from 13 to 64, as said below
- cotangent: bfloat16 [192, 64, 768], P('dp'), may hold values from -6 to 6
- ln1_gain: float32 [768], replicated, may hold values from 0.5 to 1.5
- ln1_bias: float32 [768], replicated, may hold values from -3 to 3
- w_qkv: bfloat16 [3, 768, 768], P(None, 'dp', 'tensor'), may hold values from -0.21875 to 0.21875
- b_qkv: float32 [2, 768], P(None, 'tensor'), may hold values from -3 to 3
- w_out: bfloat16 [768, 768], P('tensor', 'dp'), may hold values from -0.875 to 0.875
- b_out: float32 [768], replicated, may hold values from -3 to 3
- ln2_gain: float32 [768], replicated, may hold values from 0.5 to 1.5
- ln2_bias: float32 [768], replicated, may hold values from -3 to 3
- w_up: bfloat16 [768, 3072], P('dp', 'tensor'), may hold values from -0.21875 to 0.21875
- b_up: float32 [3072], P('tensor'), may hold values from -3 to 3
- w_down: bfloat16 [3072, 768], P('tensor', 'dp'), may hold values from -0.109375 to 0.109375
- b_down: float32 [768], replicated, may hold values from -3 to 3
Outputs:
- block_output: bfloat16 [192, 64, 768], P('dp')
- patches_grad: bfloat16 [192, 64, 768], P('dp')
- ln1_gain_grad: float32 [768], replicated
- ln1_bias_grad: float32 [768], replicated
- w_qkv_grad: float32 [3, 768, 768], P(None, 'dp', 'tensor')
- b_qkv_grad: float32 [2, 768], P(None, 'tensor')
- w_out_grad: float32 [768, 768], P('tensor', 'dp')
- b_out_grad: float32 [768], replicated
- ln2_gain_grad: float32 [768], replicated
- ln2_bias_grad: float32 [768], replicated
- w_up_grad: float32 [768, 3072], P('dp', 'tensor')
- b_up_grad: float32 [3072], P('tensor')
- w_down_grad: float32 [3072, 768], P('tensor', 'dp')
- b_down_grad: float32 [768], replicated
Inputs may be any that keep to these rules, and one draw needn't show every extreme that they name: visible[s] is the number of visible patches of sample s; some sample has exactly 64 and some exactly 13.
All inputs are finite; a program needn't handle non-finite values.
Results may differ from a plain program's by a relative error of at most 0.015.
Values may be sent and summed in bfloat16 or wider, within the bound.
No kernel may reach another device: no remote copies, remote signals or barrier semaphores. Data moves between devices by JAX's collectives and lax.ppermute only.
A program may use at most 128 MiB of HBM per device.

v0:
```python
import enum
import functools

import jax
import jax.numpy as jnp
from jax import lax
from jax.experimental import pallas as pl
from jax.experimental.pallas import tpu as pltpu
from jax.sharding import PartitionSpec as P

HD = 64
VIS = 64
EPS = 1e-06
BF = jnp.bfloat16
F32 = jnp.float32
NEG = -1000000000.0
PAIR = 2 * VIS
PLACE = 6
X, Y, Z_LOW, Z_HIGH = 1, 3, 4, 5

class K(enum.Enum):
    y_bias = enum.auto()
    z2_att = enum.auto()
    z2_dn = enum.auto()
    z2_up = enum.auto()
    p_att = enum.auto()
    z1_att = enum.auto()
    a_att = enum.auto()
    x_att = enum.auto()
    y_att = enum.auto()
    p_dn = enum.auto()
    z1_dn = enum.auto()
    p_up = enum.auto()
    x_up = enum.auto()
    c_att = enum.auto()
    a_dn = enum.auto()
    x_dn = enum.auto()
    px_up = enum.auto()
    z1_up = enum.auto()
    c_x_att = enum.auto()
    xy_att = enum.auto()
    c_y_att = enum.auto()
    c_xy_att = enum.auto()
    small = enum.auto()
    c_dn1 = enum.auto()
    c_dn2 = enum.auto()
    a_up = enum.auto()
    c_up = enum.auto()
    attend0 = enum.auto()
    feed0 = enum.auto()
    y_gn2_0 = enum.auto()
    attend1 = enum.auto()
    feed1 = enum.auto()
    y_gn2_1 = enum.auto()
    grad_dn = enum.auto()
    gc_dn = enum.auto()
    grad_up = enum.auto()
    gc_up = enum.auto()
    add_c_dn = enum.auto()
    gx_dn = enum.auto()
    add_c_up = enum.auto()
    gx_up = enum.auto()
    back0 = enum.auto()
    add_x_dn = enum.auto()
    gz1_dn = enum.auto()
    back1 = enum.auto()
    grad_qkv = enum.auto()
    gc_qkv = enum.auto()
    add_c_qkv = enum.auto()
    gx_qkv = enum.auto()
    grad_out = enum.auto()
    gc_out = enum.auto()
    rows0 = enum.auto()
    down0 = enum.auto()
    y_down0 = enum.auto()
    add_z_dn = enum.auto()
    gz2_dn = enum.auto()
    rows1 = enum.auto()
    down1 = enum.auto()
    y_down1 = enum.auto()
    c_sums = enum.auto()
    add_x_up = enum.auto()
    gz1_up = enum.auto()
    add_x_qkv = enum.auto()
    gz1_qkv = enum.auto()
    add_c_out = enum.auto()
    gz1_out = enum.auto()
    add_z_out = enum.auto()
    gz2_out = enum.auto()
    add_z_up = enum.auto()
    gz2_up = enum.auto()
    add_z_qkv = enum.auto()
    gz2_qkv = enum.auto()
    add_x_out = enum.auto()
    gx_out = enum.auto()
    finish_dn = enum.auto()
    finish_up = enum.auto()
    finish_out = enum.auto()
    out0 = enum.auto()
    out1 = enum.auto()
    finish_qkv = enum.auto()


MIB = 1024 * 1024
TILE = 256

NN = (((1,), (0,)), ((), ()))
NT = (((1,), (1,)), ((), ()))
TN = (((0,), (0,)), ((), ()))


def mm(left, right, dims=NN):
    return lax.dot_general(left, right, dims, preferred_element_type=F32)


def rows_of(t):
    return pl.ds(t * PAIR, PAIR)


def tile_rows(t):
    return pl.ds(pl.multiple_of(t * PAIR, PAIR), PAIR)


def norm_stats(v):
    mean = jnp.mean(v, axis=-1, keepdims=True)
    centred = v - mean
    inv = lax.rsqrt(jnp.mean(centred * centred, axis=-1, keepdims=True) + EPS)
    return centred * inv, inv


def low_lanes(shape):
    return lax.broadcasted_iota(jnp.int32, shape, 1) < HD


def two_heads(block, low):
    zero = jnp.zeros_like(block)
    return jnp.concatenate([jnp.where(low, block, zero), jnp.where(low, zero, block)], axis=0)


def col_sum(v):
    return jnp.sum(v, axis=0, keepdims=True)


def lay_out(where, parts, buf):
    blocks, r, _ = parts[0].shape
    for b in range(blocks):
        for i, part in enumerate(parts):
            cc = where[2] if i < len(parts) // 2 else 1 - where[2]
            if len(parts) == 2:
                place = b * 2 + cc
            else:
                xx = where[1] if i % 2 == 0 else 1 - where[1]
                place = (b * 2 + xx) * 2 + cc
            buf[pl.ds(pl.multiple_of(place * r, 16), r), :] = part[b]


def attend_kernel(base, at, n_alias, counts, where, x, small, *refs):
    if len(refs[0].shape) == 3 and refs[0].dtype == BF and refs[0].shape[0] == 2:
        w, refs = refs[0], refs[1:]
        outs, (mixed,) = refs[n_alias : n_alias + 8], refs[n_alias + 8 :]
    else:
        parts, refs = refs[:8], refs[8:]
        outs, (w, mixed) = refs[n_alias : n_alias + 8], refs[n_alias + 8 :]
        lay_out(where, parts[:4], w.at[where[3]])
        lay_out(where, parts[4:], w.at[1 - where[3]])
    norm_o, q_o, k_o, v_o, probs_o, mixed_o, mid_o, norm2_o = outs
    g1, b1, b_q, b_v, b_out, g2, b2 = (small.at[:, at[i] : at[i + 1]] for i in range(7))
    rows, d = x.shape
    e = mixed_o.shape[1]
    for t in range(rows // PAIR):
        xhat, _ = norm_stats(x[rows_of(t), :].astype(F32))
        norm_o[rows_of(t), :] = (xhat * g1[...] + b1[...]).astype(BF)
    n = norm_o[...]
    for h in range(2):
        half = slice(h * e, (h + 1) * e)
        q_o[:, half] = (mm(n, w[h, :, 0:e]) + b_q[:, half]).astype(BF)
        k_o[:, half] = mm(n, w[h, :, e : 2 * e]).astype(BF)
        v_o[:, half] = (mm(n, w[h, :, 2 * e : 3 * e]) + b_v[:, half]).astype(BF)
    low = low_lanes((PAIR, PAIR))
    row = lax.broadcasted_iota(jnp.int32, (PAIR, PAIR), 0)
    col = lax.broadcasted_iota(jnp.int32, (PAIR, PAIR), 1)
    pairs = 2 * e // PAIR
    for t in range(rows // PAIR):
        first = counts[base + 2 * t]
        second = counts[base + 2 * t + 1]
        valid = ((row < VIS) & (col < jnp.minimum(first, VIS))) | (
            (row >= VIS) & (col >= VIS) & (col < VIS + second)
        )
        for p in range(pairs):
            lanes = pl.ds(p * PAIR, PAIR)
            q2 = q_o[rows_of(t), lanes]
            kc = two_heads(k_o[rows_of(t), lanes], low)
            vc = two_heads(v_o[rows_of(t), lanes], low)
            scores = mm(q2, kc, NT) * (HD**-0.5)
            for h in range(2):
                s = jnp.where(valid, scores[:, h * PAIR : (h + 1) * PAIR], NEG)
                ex = jnp.exp(s - jnp.max(s, axis=-1, keepdims=True))
                probs_o[t * pairs + p, :, pl.ds(h * PAIR, PAIR)] = ex / jnp.sum(
                    ex, axis=-1, keepdims=True
                )
            pb = probs_o[t * pairs + p].astype(BF)
            mixed[2 * p // pairs, rows_of(t), pl.ds(p % (pairs // 2) * PAIR, PAIR)] = mm(
                pb, vc
            ).astype(BF)
    mixed_o[...] = mixed[where[3]]
    for t in range(rows // PAIR):
        r = rows_of(t)
        proj = mm(mixed[0, r, :], w[0, :, 3 * e : 4 * e], NT)
        proj = proj + mm(mixed[1, r, :], w[1, :, 3 * e : 4 * e], NT)
        middle = x[r, :].astype(F32) + (proj + b_out[...])
        mid_o[r, :] = middle
        xhat, _ = norm_stats(middle)
        norm2_o[r, :] = (xhat * g2[...] + b2[...]).astype(BF)


def feed_kernel(at, up_at, first, n_alias, n2, small, cot, *refs):
    if first and refs[0].shape == (PLACE,):
        parts_up, refs = (refs[0], refs[1:3]), refs[3:]
        parts_dn, refs = (refs[0], refs[1:5]), refs[5:]
        w_up, w_dn = refs[n_alias + 4 : n_alias + 6]
        lay_out(*parts_up, w_up)
        lay_out(*parts_dn, w_dn)
    else:
        w_up, w_dn, *refs = refs
    b_up = small.at[:, up_at : up_at + w_up.shape[1]]
    if not first:
        sums, *refs = refs
    act_o, gu_o, gn_o, sums_o = refs[n_alias : n_alias + 4]
    f = w_up.shape[1]
    if first:
        sums_o[...] = jnp.zeros_like(sums_o)
    else:
        sums_o[...] = sums[...]
    for j in range(f // TILE):
        c = pl.ds(j * TILE, TILE)
        u = mm(n2[...], w_up[:, c]) + b_up[:, c]
        ga = mm(cot[...], w_dn[:, c])
        cdf = 0.5 * (1.0 + lax.erf(u * (0.5**0.5)))
        pdf = jnp.exp(u * u * -0.5) * 0.3989422804014327
        act_o[:, c] = (u * cdf).astype(BF)
        gu = (ga * (cdf + u * pdf)).astype(BF)
        gu_o[:, c] = gu
        lo = at[7] + j * TILE
        sums_o[:, lo : lo + TILE] += col_sum(gu.astype(F32))
    gn_o[...] = mm(gu_o[...], w_up[...], NT).astype(BF)


def down_kernel(n_alias, act, w_dn, *refs):
    refs[n_alias][...] = mm(act[...], w_dn[...], NT).astype(BF)


def norm_back(grad, gain, xhat, inv):
    t = grad * gain
    return inv * (
        t
        - jnp.mean(t, axis=-1, keepdims=True)
        - xhat * jnp.mean(t * xhat, axis=-1, keepdims=True)
    )


def back_kernel(at, gain, n_alias, middle, own, other, cot, small, q, k, v, probs, sums, w, *refs):
    gp_o, gqkv_o, sums_o = refs[n_alias : n_alias + 3]
    (gmix,) = refs[n_alias + 3 :]
    rows, d = cot.shape
    gain2 = small.at[:, gain : gain + d]
    e = gmix.shape[1] // 2
    sums_o[...] = sums[...]
    out_at, g2_at, b2_at = (at[i] for i in (4, 5, 6))
    for t in range(rows // PAIR):
        r = rows_of(t)
        gn = own[r, :].astype(F32) + other[r, :].astype(F32)
        xhat, inv = norm_stats(middle[r, :])
        gp = (cot[r, :].astype(F32) + norm_back(gn, gain2[...], xhat, inv)).astype(BF)
        gp_o[r, :] = gp
        sums_o[:, g2_at : g2_at + d] += col_sum(gn * xhat)
        sums_o[:, b2_at : b2_at + d] += col_sum(gn)
        sums_o[:, out_at : out_at + d] += col_sum(gp.astype(F32))
    for h in range(2):
        gmix[:, h * e : (h + 1) * e] = mm(gp_o[...], w[h, :, 3 * e : 4 * e]).astype(BF)
    low = low_lanes((PAIR, PAIR))
    pairs = 2 * e // PAIR

    @pl.loop(0, rows // PAIR)
    def _(t):
        r = tile_rows(t)
        for p in range(pairs):
            lanes = pl.ds(p * PAIR, PAIR)
            first = 2 * p // pairs * 3 * e + p % (pairs // 2) * PAIR
            q2 = q[r, lanes]
            g2 = gmix[r, lanes]
            kc = two_heads(k[r, lanes], low)
            vc = two_heads(v[r, lanes], low)
            pr = probs[t * pairs + p]
            gprob = mm(g2, vc, NT)
            prod = pr * gprob
            tot = jnp.concatenate(
                [
                    jnp.broadcast_to(
                        jnp.sum(prod[:, i * PAIR : (i + 1) * PAIR], axis=-1, keepdims=True),
                        (PAIR, PAIR),
                    )
                    for i in range(2)
                ],
                axis=1,
            )
            gs = (pr * (gprob - tot)).astype(BF)
            gq = mm(gs, kc) * (HD**-0.5)
            gk = mm(gs, q2, TN)
            gv = mm(pr.astype(BF), g2, TN)
            gqkv_o[r, pl.ds(first, PAIR)] = gq.astype(BF)
            gqkv_o[r, pl.ds(first + e, PAIR)] = (
                jnp.where(low, gk[:PAIR], gk[PAIR:]) * (HD**-0.5)
            ).astype(BF)
            gqkv_o[r, pl.ds(first + 2 * e, PAIR)] = jnp.where(low, gv[:PAIR], gv[PAIR:]).astype(BF)


def rows_kernel(at, gain, n_alias, where, gqkv, w, x, gp, cot, small, sums, *refs):
    rows_o, sums_o = refs[n_alias : n_alias + 2]
    (gn1,) = refs[n_alias + 2 :]
    rows, d = x.shape
    e = gqkv.shape[1] // 6
    gain1 = small.at[:, gain : gain + d]
    sums_o[...] = sums[...]
    g1_at, b1_at, q_at, v_at, down_at = (at[i] for i in (0, 1, 2, 3, 8))
    mine = pl.multiple_of(where[Y] * 3 * e, PAIR)
    sums_o[:, q_at : q_at + e] += col_sum(gqkv[:, pl.ds(mine, e)].astype(F32))
    mine = pl.multiple_of(where[Y] * 3 * e + 2 * e, PAIR)
    sums_o[:, v_at : v_at + e] += col_sum(gqkv[:, pl.ds(mine, e)].astype(F32))
    sums_o[:, down_at : down_at + d] += col_sum(cot[...].astype(F32))
    gn1[...] = mm(gqkv[:, : 3 * e], w[0, :, 0 : 3 * e], NT) + mm(
        gqkv[:, 3 * e :], w[1, :, 0 : 3 * e], NT
    )
    for t in range(rows // PAIR):
        r = rows_of(t)
        xhat, inv = norm_stats(x[r, :].astype(F32))
        gn = gn1[r, :]
        rows_o[r, :] = (gp[r, :].astype(F32) + norm_back(gn, gain1[...], xhat, inv)).astype(BF)
        sums_o[:, g1_at : g1_at + d] += col_sum(gn * xhat)
        sums_o[:, b1_at : b1_at + d] += col_sum(gn)


def chunk_spec(shape, ch):
    return pl.BlockSpec(
        shape, lambda i: (ch,) + (0,) * (len(shape) - 1), pipeline_mode=pl.Buffered(1)
    )


def whole_spec(shape):
    return pl.BlockSpec(shape, lambda i: (0,) * len(shape), pipeline_mode=pl.Buffered(1))


SMEM_SPEC = pl.BlockSpec(memory_space=pltpu.SMEM)


def call(kernel, ch, n_ch, inputs, kept, fresh, scratch=(), name=None, mib=8):
    deps = need(name)
    in_specs, args = [], []
    for arr, kind in inputs:
        args.append(arr)
        if kind == "s":
            in_specs.append(SMEM_SPEC)
        elif kind == "c":
            in_specs.append(chunk_spec((arr.shape[0] // n_ch,) + arr.shape[1:], ch))
        else:
            in_specs.append(whole_spec(arr.shape))
    out_shapes, out_specs, aliases = [], [], {}
    for i, (shape, dtype, previous) in enumerate(kept):
        out_shapes.append(jax.ShapeDtypeStruct(shape, dtype))
        out_specs.append(chunk_spec((shape[0] // n_ch,) + shape[1:], ch))
        if previous is not None:
            aliases[len(args)] = i
            args.append(previous)
            in_specs.append(pl.BlockSpec(memory_space=pl.ANY))
    args += list(deps)
    in_specs += [pl.BlockSpec(memory_space=pl.ANY)] * len(deps)
    for shape, dtype in fresh:
        out_shapes.append(jax.ShapeDtypeStruct(shape, dtype))
        out_specs.append(whole_spec(shape))
    out = pl.pallas_call(
        functools.partial(kernel, len(aliases) + len(deps)),
        grid=(1,),
        in_specs=in_specs,
        out_specs=out_specs,
        out_shape=out_shapes,
        scratch_shapes=list(scratch),
        input_output_aliases=aliases,
        compiler_params=pltpu.CompilerParams(vmem_limit_bytes=mib * MIB),
        cost_estimate=cost(name),
        name=name.name,
    )(*args)
    return made(name, out)


WEIGHT = {
    K.grad_dn: 15,
    K.add_z_out: 2,
    K.xy_att: 15,
    K.back1: 2,
    K.finish_qkv: 40,
    K.back0: 15,
    K.a_up: 15,
    K.feed0: 15,
    K.out1: 40,
    K.add_x_dn: 40,
    K.add_z_dn: 5,
    K.add_x_qkv: 5,
    K.add_z_qkv: 15,
    K.add_c_up: 40,
    K.add_x_out: 2,
    K.add_c_out: 15,
    K.grad_qkv: 2,
}
ORDER = {
    K.gc_up: [K.y_gn2_0, K.c_dn1],
    K.back0: [K.add_c_dn],
    K.a_att: [K.p_up],
    K.z2_dn: [K.y_bias],
    K.z1_up: [K.a_dn],
    K.z2_att: [K.y_bias],
    K.add_c_up: [K.grad_dn],
    K.out0: [K.finish_dn],
    K.gc_dn: [K.y_gn2_0],
    K.xy_att: [K.z2_up],
    K.out1: [K.gz2_dn],
    K.finish_dn: [K.add_z_qkv],
    K.add_c_out: [K.gz1_up],
    K.attend0: [K.c_dn2],
    K.add_x_up: [K.grad_out],
    K.add_z_qkv: [K.add_z_up],
    K.down1: [K.gx_dn],
    K.grad_dn: [K.a_up],
    K.gc_out: [K.back0],
    K.gz2_up: [K.add_z_out],
    K.add_z_dn: [K.y_down0],
}


def cost(name):
    return pl.CostEstimate(
        flops=int(WEIGHT.get(name, 0) * 1.1e9), bytes_accessed=0, transcendentals=0
    )


MADE = {}


def need(name):
    return tuple(MADE[n] for n in ORDER.get(name, ()) if n in MADE)


def made(name, out):
    MADE[name] = out[-1] if isinstance(out, (list, tuple)) else out
    return out


def after(x, *deps):
    return lax.optimization_barrier((x,) + deps)[0] if deps else x


class Links:
    def __init__(self, n):
        self.n = n
        self.depth = n // 4
        me = lax.axis_index("dp")
        self.core, self.x, self.z = me % 2, (me // 2) % 2, me // 4
        self.y = lax.axis_index("tensor")
        self.where = jnp.stack(
            [self.z, self.x, self.core, self.y, self.z % 2, self.z // 2]
        ).astype(jnp.int32)

    def move(self, name, v, axis, pairs):
        return made(name, lax.ppermute(after(v, *need(name)), axis, pairs))

    def core_swap(self, name, v):
        return self.move(name, v, "dp", [(i, i ^ 1) for i in range(self.n)])

    def x_swap(self, name, v):
        return self.move(name, v, "dp", [(i, i ^ 2) for i in range(self.n)])

    def z_low(self, name, v):
        return self.move(name, v, "dp", [(i, i ^ 4) for i in range(self.n)])

    def z_high(self, name, v):
        return self.move(name, v, "dp", [(i, i ^ 8) for i in range(self.n)])

    def y_swap(self, name, v):
        return self.move(name, v, "tensor", [(0, 1), (1, 0)])


def simple(kernel, name, inputs, outs, **kw):
    deps = need(name)
    specs = [SMEM_SPEC if kind == "s" else whole_spec(a.shape) for a, kind in inputs]
    specs += [pl.BlockSpec(memory_space=pl.ANY)] * len(deps)
    n_in = len(inputs)

    def body(*refs):
        kernel(*refs[:n_in], *refs[n_in + len(deps) :], **kw)

    out = pl.pallas_call(
        body,
        grid=(1,),
        in_specs=specs,
        out_specs=[whole_spec(shape) for shape, _ in outs],
        out_shape=[jax.ShapeDtypeStruct(shape, dtype) for shape, dtype in outs],
        compiler_params=pltpu.CompilerParams(vmem_limit_bytes=8 * MIB),
        cost_estimate=cost(name),
        name=name.name,
    )(*[a for a, _ in inputs], *deps)
    return made(name, out)


def small_kernel(where, mine, got, *refs):
    out, row = refs[-1], [a[...].reshape(1, -1) for a in refs[:-1]]
    swap = where[3] == 0
    first, second = mine[...], got[...]
    first, second = jnp.where(swap, first, second), jnp.where(swap, second, first)
    row[2:2] = [first[0:1], second[0:1], first[1:2], second[1:2]]
    at = 0
    for a in row:
        out[:, at : at + a.shape[1]] = a
        at += a.shape[1]


def index_of(i, bit, inner):
    return (i // inner * 2 + bit) * inner + i % inner


def merge_kernel(where, own, got, out, axis, inner):
    bit = where[axis]
    if len(own.shape) == 2:
        out[bit] = own[...]
        out[1 - bit] = got[...]
        return
    for i in range(own.shape[0]):
        out[index_of(i, bit, inner)] = own[i]
        out[index_of(i, 1 - bit, inner)] = got[i]


def merge(links, name, own, got, axis, inner=1):
    shape = (2 * own.size // (own.shape[-1] * own.shape[-2]),) + own.shape[-2:]
    inputs = [(links.where, "s"), (own, "w"), (got, "w")]
    return simple(merge_kernel, name, inputs, [(shape, BF)], axis=axis, inner=inner)[0]


def grad_kernel(where, left, right, keep, send):
    n, r, width = keep.shape
    if right.shape[1] == width:
        g = mm(left[...], right[...], TN)
    else:
        mine = pl.multiple_of(where[Y] * width, PAIR)
        g = mm(left[...], right[:, pl.ds(mine, width)], TN)
    g = g.astype(BF).reshape(n, 2, r, width)
    for c in range(2):

        @pl.when(where[2] == c)
        def _(g=g, c=c):
            keep[...] = g[:, c]
            send[...] = g[:, 1 - c]


def weight_grad(links, name, left, right, width):
    deps = need(name)
    rows, d = left.shape
    n, r = links.n // 2, d // links.n
    steps = 2

    def body(*refs):
        grad_kernel(*refs[:3], *refs[3 + len(deps) :])

    out = pl.pallas_call(
        body,
        grid=(steps,),
        in_specs=[
            SMEM_SPEC,
            pl.BlockSpec((rows, d // steps), lambda i: (0, i)),
            whole_spec(right.shape),
        ]
        + [pl.BlockSpec(memory_space=pl.ANY)] * len(deps),
        out_specs=[pl.BlockSpec((n // steps, r, width), lambda i: (i, 0, 0))] * 2,
        out_shape=[jax.ShapeDtypeStruct((n, r, width), BF)] * 2,
        compiler_params=pltpu.CompilerParams(vmem_limit_bytes=20 * MIB),
        cost_estimate=cost(name),
        name=name.name,
    )(links.where, left, right, *deps)
    return made(name, out)


def halve_kernel(where, mine, got, keep, send, axis):
    bit = where[axis]
    if len(keep.shape) == 2:
        keep[...] = mine[bit].astype(F32) + got[bit].astype(F32)
        send[...] = mine[1 - bit] + got[1 - bit]
        return
    for i in range(keep.shape[0]):
        a, b = 2 * i + bit, 2 * i + 1 - bit
        keep[i] = mine[a] + got[a]
        send[i] = mine[b] + got[b]


def halve(links, name, mine, got, axis):
    n = mine.shape[0] // 2
    shape = mine.shape[1:] if n == 1 else (n,) + mine.shape[1:]
    inputs = [(links.where, "s"), (mine, "w"), (got, "w")]
    outs = [(shape, F32 if n == 1 else BF), (shape, BF)]
    return simple(halve_kernel, name, inputs, outs, axis=axis)


EXTRA = 48


def pack(v, ref, row):
    width = ref.shape[-1]
    ref[row:, :] = jnp.zeros((EXTRA, width), BF)
    for i in range(v.shape[1] // width):
        high = v[:, i * width : (i + 1) * width].astype(BF)
        low = (v[:, i * width : (i + 1) * width] - high.astype(F32)).astype(BF)
        ref[row + i : row + i + 1, :] = high
        ref[row + EXTRA // 2 + i : row + EXTRA // 2 + i + 1, :] = low


def unpack(ref, row, n):
    half = EXTRA // 2
    v = ref[row : row + half, :].astype(F32) + ref[row + half :, :].astype(F32)
    return jnp.concatenate([v[i : i + 1, :] for i in range(n)], axis=1)


def rounded(v):
    high = v.astype(BF).astype(F32)
    return high + (v - high).astype(BF).astype(F32)


def add_core_out_kernel(where, mine, got, sums, sums_got, keep, send, total):
    depth, r, _ = keep.shape
    v = sums[...] + sums_got[...]
    total[...] = rounded(v)
    for i in range(depth):
        a, b = index_of(i, where[Z_LOW], 2), index_of(i, 1 - where[Z_LOW], 2)
        keep[i] = mine[a] + got[a]
        send[i * r : (i + 1) * r, :] = mine[b] + got[b]
    pack(v, send, depth * r)


def add_core_out(links, mine, got, sums, sums_got):
    _, r, e = mine.shape
    inputs = [(links.where, "s")] + [(a, "w") for a in (mine, got, sums, sums_got)]
    outs = [((links.depth, r, e), BF), ((links.depth * r + EXTRA, e), BF), (sums.shape, F32)]
    return simple(add_core_out_kernel, K.add_c_out, inputs, outs)


def halve_sums_kernel(where, mine, got, sums, keep, send, total, axis, inner):
    bit = where[axis]
    n, r, e = mine.shape
    v = sums[...] + unpack(got, n * r, sums.shape[1] // e)
    total[...] = rounded(v)
    for i in range(n // 2):
        a, b = index_of(i, bit, inner), index_of(i, 1 - bit, inner)
        keep[i] = mine[a] + got[pl.ds(pl.multiple_of(a * r, 16), r), :]
        send[i * r : (i + 1) * r, :] = mine[b] + got[pl.ds(pl.multiple_of(b * r, 16), r), :]
    pack(v, send, n // 2 * r)


def halve_sums(links, name, mine, got, sums, axis, inner):
    n, r, e = mine.shape
    inputs = [(links.where, "s"), (mine, "w"), (got, "w"), (sums, "w")]
    outs = [((n // 2, r, e), BF), ((n // 2 * r + EXTRA, e), BF), (sums.shape, F32)]
    return simple(halve_sums_kernel, name, inputs, outs, axis=axis, inner=inner)


def finish_out_kernel(mine, got, sums, g_out, *outs, cuts, pair):
    _, r, e = mine.shape
    g_out[...] = mine[0].astype(F32) + got[0:r, :].astype(F32)
    v = sums[...] + unpack(got, r, sums.shape[1] // e)
    for i, out in enumerate(outs):
        a, b = cuts[i], cuts[i + 1]
        if i == pair:
            out[0:1, :] = v[:, a : (a + b) // 2]
            out[1:2, :] = v[:, (a + b) // 2 : b]
        else:
            out[...] = v[0, a:b]


def finish_out(links, mine, got, sums, cuts, pair):
    _, r, e = mine.shape
    sizes = [(b - a,) for a, b in zip(cuts, cuts[1:])]
    sizes[pair] = (2, sizes[pair][0] // 2)
    outs = [((r, e), F32)] + [(size, F32) for size in sizes]
    inputs = [(a, "w") for a in (mine, got, sums)]
    return simple(finish_out_kernel, K.finish_out, inputs, outs, cuts=cuts, pair=pair)


def finish_kernel(mine, got, out):
    total = mine[...] + got[...].astype(F32)
    if len(out.shape) == 3:
        e = out.shape[2]
        for t in range(3):
            out[t] = total[:, t * e : (t + 1) * e]
    else:
        out[...] = total


def finish(name, mine, got, shape):
    return simple(finish_kernel, name, [(mine, "w"), (got, "w")], [(shape, F32)])[0]


def out_kernel(bias_at, n_alias, middle, own, other, small, *refs):
    bias = small.at[:, bias_at : bias_at + middle.shape[1]]
    out = refs[n_alias]
    for t in range(middle.shape[0] // PAIR):
        r = rows_of(t)
        down = own[r, :].astype(F32) + other[r, :].astype(F32)
        out[r, :] = (middle[r, :] + (down + bias[...])).astype(BF)


def local(
    n_dp,
    patches,
    visible,
    cotangent,
    ln1_gain,
    ln1_bias,
    w_qkv,
    b_qkv,
    w_out,
    b_out,
    ln2_gain,
    ln2_bias,
    w_up,
    b_up,
    w_down,
    b_down,
):
    MADE.clear()
    samples, vis, d = patches.shape
    rows = samples * vis
    e = w_qkv.shape[2]
    f = w_up.shape[1]
    n_ch = 2
    per = rows // n_ch
    fast = n_dp == 16
    links = Links(n_dp)

    at = [0]
    for size in (d, d, e, e, d, d, d, f, d):
        at.append(at[-1] + size)
    n_sums = -(-at[-1] // e) * e
    cuts = [0, d, 2 * d, 2 * d + 2 * e] + at[5:]
    s_at = [0]
    for size in (d, d, 2 * e, 2 * e, d, d, d, f, d):
        s_at.append(s_at[-1] + size)
    b_got = links.y_swap(K.y_bias, b_qkv)
    small = simple(
        small_kernel,
        K.small,
        [(links.where, "s")]
        + [
            (a, "w")
            for a in (b_qkv, b_got, ln1_gain, ln1_bias, b_out, ln2_gain, ln2_bias, b_up, b_down)
        ],
        [((1, s_at[-1]), F32)],
    )[0]
    x = patches.reshape(rows, d)
    cot = cotangent.reshape(rows, d)
    groups = rows // PAIR * (2 * e // PAIR)

    own_att = jnp.concatenate([w_qkv[0], w_qkv[1], w_qkv[2], w_out.T], axis=1)
    own_dn = w_down.T
    if fast:
        z_att = links.z_high(K.z2_att, own_att)
        z_dn = links.z_high(K.z2_dn, own_dn)
        z_up = links.z_high(K.z2_up, w_up)
        p_att = merge(links, K.p_att, own_att, z_att, Z_HIGH)
        a_att = merge(links, K.a_att, p_att, links.z_low(K.z1_att, p_att), Z_LOW)
        x_att = links.x_swap(K.x_att, a_att)
        y_att = links.y_swap(K.y_att, a_att)
        p_dn = merge(links, K.p_dn, own_dn, z_dn, Z_HIGH)
        z_dn = links.z_low(K.z1_dn, p_dn)
        p_up = merge(links, K.p_up, w_up, z_up, Z_HIGH)
        x_up = links.x_swap(K.x_up, p_up)
        c_a = links.core_swap(K.c_att, a_att)
        a_dn = merge(links, K.a_dn, p_dn, z_dn, Z_LOW)
        x_dn = links.x_swap(K.x_dn, a_dn)
        p_up = merge(links, K.px_up, p_up, x_up, X)
        z_up = links.z_low(K.z1_up, p_up)
        c_x = links.core_swap(K.c_x_att, x_att)
        xy_att = links.y_swap(K.xy_att, x_att)
        c_y = links.core_swap(K.c_y_att, y_att)
        c_xy = links.core_swap(K.c_xy_att, xy_att)
        w_att = [(a, "w") for a in (a_att, x_att, c_a, c_x, y_att, xy_att, c_y, c_xy)]
    else:
        w_att, w_upf, w_dnf = (
            lax.all_gather(w, "dp", axis=0, tiled=True) for w in (own_att, w_up, own_dn)
        )
        w_att = [(lax.all_gather(w_att, "tensor", axis=0), "w")]
        w_feed = [(w_upf, "w"), (w_dnf, "w")]

    def attend(ch, kept, w_att):
        lays = len(w_att) > 1
        return call(
            functools.partial(attend_kernel, ch * (samples // n_ch), s_at),
            ch,
            n_ch,
            [(visible, "s"), (links.where, "s"), (x, "c"), (small, "w")] + w_att,
            [
                ((rows, d), BF, kept[0]),
                ((rows, 2 * e), BF, kept[1]),
                ((rows, 2 * e), BF, kept[2]),
                ((rows, 2 * e), BF, kept[3]),
                ((groups, PAIR, 2 * PAIR), F32, kept[4]),
                ((rows, e), BF, kept[5]),
                ((rows, d), F32, kept[6]),
                ((rows, d), BF, kept[7]),
            ],
            [((2, d, 4 * e), BF)] if lays else [],
            scratch=[pltpu.VMEM((2, per, e), BF)],
            name=(K.attend0, K.attend1)[ch],
            mib=20,
        )

    def feed(ch, kept, sums, n2, w_feed):
        lays = len(w_feed) > 2
        return call(
            functools.partial(feed_kernel, at, s_at[7], ch == 0),
            ch,
            n_ch,
            [(n2, "c"), (small, "w"), (cot, "c")] + w_feed + ([] if ch == 0 else [(sums, "w")]),
            [((rows, f), BF, kept[0]), ((rows, f), BF, kept[1])],
            [((per, d), BF), ((1, n_sums), F32)] + ([((d, f), BF)] * 2 if lays else []),
            name=(K.feed0, K.feed1)[ch],
            mib=20,
        )

    def back(ch, kept, sums):
        return call(
            functools.partial(back_kernel, at, s_at[5]),
            ch,
            n_ch,
            [
                (middle, "c"),
                (gn2[ch], "w"),
                (gn2_got[ch], "w"),
                (cot, "c"),
                (small, "w"),
                (q, "c"),
                (k, "c"),
                (v, "c"),
                (probs, "c"),
                (sums, "w"),
                (w_both, "w"),
            ],
            [((rows, d), BF, kept[0]), ((rows, 6 * e), BF, kept[1])],
            [((1, n_sums), F32)],
            scratch=[pltpu.VMEM((per, 2 * e), BF)],
            name=(K.back0, K.back1)[ch],
            mib=20,
        )

    def to_rows(ch, kept, sums):
        return call(
            functools.partial(rows_kernel, at, s_at[0]),
            ch,
            n_ch,
            [
                (links.where, "s"),
                (grad_qkv, "c"),
                (w_both, "w"),
                (x, "c"),
                (grad_proj, "c"),
                (cot, "c"),
                (small, "w"),
                (sums, "w"),
            ],
            [((rows, d), BF, kept)],
            [((1, n_sums), F32)],
            scratch=[pltpu.VMEM((per, d), F32)],
            name=(K.rows0, K.rows1)[ch],
            mib=16,
        )

    if fast:
        c_dn = [links.core_swap(K.c_dn1, a_dn), links.core_swap(K.c_dn2, x_dn)]
        a_up = merge(links, K.a_up, p_up, z_up, Z_LOW, 2)
        w_feed = [(links.where, "s"), (a_up, "w"), (links.core_swap(K.c_up, a_up), "w")]
        w_feed += [(links.where, "s")] + [(a, "w") for a in (a_dn, x_dn, *c_dn)]
    held, kept, sums = [None] * 8, [None] * 2, None
    gn2, gn2_got = [None] * n_ch, [None] * n_ch
    for ch in range(n_ch):
        held = attend(ch, held, w_att)
        if fast and ch == 0:
            *held, w_both = held
            w_att = [(w_both, "w")]
        *kept, gn2[ch], sums, a, b = list(
            feed(ch, kept, sums, held[7], w_feed)
        ) + [None] * (0 if fast and ch == 0 else 2)
        if fast and ch == 0:
            w_feed = [(a, "w"), (b, "w")]
        gn2_got[ch] = links.y_swap((K.y_gn2_0, K.y_gn2_1)[ch], gn2[ch])
    w_both = w_att[0][0]
    norm1, q, k, v, probs, mixed, middle, norm2 = held
    active, grad_up = kept
    if fast:
        k_dn, s_dn = weight_grad(links, K.grad_dn, cot, active, f)
        c_dn = links.core_swap(K.gc_dn, s_dn)
        k_up, s_up = weight_grad(links, K.grad_up, norm2, grad_up, f)
        c_up = links.core_swap(K.gc_up, s_up)
        k_dn, s_dn = halve(links, K.add_c_dn, k_dn, c_dn, X)
        x_dn = links.x_swap(K.gx_dn, s_dn)
        k_up, s_up = halve(links, K.add_c_up, k_up, c_up, X)
        x_up = links.x_swap(K.gx_up, s_up)

    kept = [None] * 2
    for ch in range(n_ch):
        *kept, sums = back(ch, kept, sums)
        if fast and ch == 0:
            k_dn, s_dn = halve(links, K.add_x_dn, k_dn, x_dn, Z_LOW)
            z_dn = links.z_low(K.gz1_dn, s_dn)
    grad_proj, grad_qkv = kept
    if fast:
        k_qkv, s_qkv = weight_grad(links, K.grad_qkv, norm1, grad_qkv, 3 * e)
        c_qkv = links.core_swap(K.gc_qkv, s_qkv)
    if fast:
        k_qkv, s_qkv = halve(links, K.add_c_qkv, k_qkv, c_qkv, X)
        x_qkv = links.x_swap(K.gx_qkv, s_qkv)
        k_out, s_out = weight_grad(links, K.grad_out, grad_proj, mixed, e)
        c_out = links.core_swap(K.gc_out, s_out)
    grad_rows = None
    down, down_got = [None] * n_ch, [None] * n_ch
    for ch in range(n_ch):
        grad_rows, sums = to_rows(ch, grad_rows, sums)
        (down[ch],) = call(
            down_kernel,
            ch,
            n_ch,
            [(active, "c"), w_feed[1]],
            [],
            [((per, d), BF)],
            name=(K.down0, K.down1)[ch],
            mib=10,
        )
        down_got[ch] = links.y_swap((K.y_down0, K.y_down1)[ch], down[ch])
        if fast and ch == 0:
            k_dn, s_dn = halve(links, K.add_z_dn, k_dn, z_dn, Z_HIGH)
            z_dn = links.z_high(K.gz2_dn, s_dn)

    if fast:
        c_sums = links.core_swap(K.c_sums, sums)
        k_up, s_up = halve(links, K.add_x_up, k_up, x_up, Z_LOW)
        z_up = links.z_low(K.gz1_up, s_up)
        k_qkv, s_qkv = halve(links, K.add_x_qkv, k_qkv, x_qkv, Z_LOW)
        z_qkv = links.z_low(K.gz1_qkv, s_qkv)
        k_out, s_out, sums = add_core_out(links, k_out, c_out, sums, c_sums)
        z_out = links.z_low(K.gz1_out, s_out)
        k_out, s_out, sums = halve_sums(links, K.add_z_out, k_out, z_out, sums, Z_HIGH, 2)
        z_out = links.z_high(K.gz2_out, s_out)
        k_up, s_up = halve(links, K.add_z_up, k_up, z_up, Z_HIGH)
        z_up = links.z_high(K.gz2_up, s_up)
        k_qkv, s_qkv = halve(links, K.add_z_qkv, k_qkv, z_qkv, Z_HIGH)
        z_qkv = links.z_high(K.gz2_qkv, s_qkv)
        k_out, s_out, sums = halve_sums(links, K.add_x_out, k_out, z_out, sums, X, 1)
        x_out = links.x_swap(K.gx_out, s_out)
        g_dn = finish(K.finish_dn, k_dn, z_dn, k_dn.shape)
        g_up = finish(K.finish_up, k_up, z_up, k_up.shape)
        g_out, *part = finish_out(links, k_out, x_out, sums, cuts, 2)
    else:
        g_dn, g_up, g_qkv, g_out = (
            lax.psum_scatter(mm(a, b, TN).astype(BF), "dp", scatter_dimension=0, tiled=True)
            for a, b in (
                (cot, active),
                (norm2, grad_up),
                (norm1, lax.dynamic_slice_in_dim(grad_qkv, links.y * 3 * e, 3 * e, axis=1)),
                (grad_proj, mixed),
            )
        )
        g_dn, g_up, g_qkv, g_out = (g.astype(F32) for g in (g_dn, g_up, g_qkv, g_out))
        g_qkv = jnp.stack([g_qkv[:, 0:e], g_qkv[:, e : 2 * e], g_qkv[:, 2 * e : 3 * e]])
        sums = lax.psum(sums, "dp")
        part = [sums[0, a:b] for a, b in zip(cuts, cuts[1:])]
        part[2] = part[2].reshape(2, e)

    output = None
    for ch in range(n_ch):
        (output,) = call(
            functools.partial(out_kernel, s_at[8]),
            ch,
            n_ch,
            [(middle, "c"), (down[ch], "w"), (down_got[ch], "w"), (small, "w")],
            [((rows, d), BF, output)],
            [],
            name=(K.out0, K.out1)[ch],
        )
    if fast:
        g_qkv = finish(K.finish_qkv, k_qkv, z_qkv, (3, k_qkv.shape[0], e))

    return (
        output.reshape(patches.shape),
        grad_rows.reshape(patches.shape),
        part[0],
        part[1],
        g_qkv,
        part[2],
        g_out.T,
        part[3],
        part[4],
        part[5],
        g_up,
        part[6],
        g_dn.T,
        part[7],
    )


def solution(mesh):
    return jax.shard_map(
        functools.partial(local, mesh.shape["dp"]),
        mesh=mesh,
        in_specs=(
            P("dp", None, None),
            P("dp"),
            P("dp", None, None),
            P(),
            P(),
            P(None, "dp", "tensor"),
            P(None, "tensor"),
            P("tensor", "dp"),
            P(),
            P(),
            P(),
            P("dp", "tensor"),
            P("tensor"),
            P("tensor", "dp"),
            P(),
        ),
        out_specs=(
            P("dp", None, None),
            P("dp", None, None),
            P(),
            P(),
            P(None, "dp", "tensor"),
            P(None, "tensor"),
            P("tensor", "dp"),
            P(),
            P(),
            P(),
            P("dp", "tensor"),
            P("tensor"),
            P("tensor", "dp"),
            P(),
        ),
        check_vma=False,
    )
```

profile of v0, /device:TPU:0, one launch (start us, length us, event | category | flops | bytes accessed | tf_op | source)
XLA Modules:
  0.0 166.8 jit_solution(17903376427838661845)
XLA Ops:
  0.7 3.0 %collective-permute-start = (f32[2,384]{1,0:T(2,128)}, f32[2,384]{1,0:T(2,128)S(1)}, u32[]{:S(2)}, u32[]{:S(2)}) collective-permute-start(f32[2,384]{1,0:T(2,128)} %refs_1_.2), channel_id=1, source_target_pairs={{0,1},{1,0},{2,3},{3,2},{4,5},{5,4},{6,7},{7,6},{8,9},{9,8},{10,11... | collective-permute-start | bytes 9224 | tf_op jit(solution)/shard_map/ppermute | solution.py:472
  3.7 2.6 %collective-permute-start.7 = (bf16[48,1536]{1,0:T(8,128)(2,1)}, bf16[48,1536]{1,0:T(8,128)(2,1)S(1)}, u32[]{:S(2)}, u32[]{:S(2)}) collective-permute-start(bf16[48,1536]{1,0:T(8,128)(2,1)} %refs_1_.3), channel_id=1, source_target_pairs={{0,16},{2,18},{4,20},{6,22},{8,24},{10,26},{12,28},{14,30},{16,0},... | collective-permute-start | bytes 442376 | tf_op jit(solution)/shard_map/ppermute | solution.py:472
  8.6 2.3 %collective-permute-start.11 = (bf16[48,1536]{1,0:T(8,128)(2,1)}, bf16[48,1536]{1,0:T(8,128)(2,1)S(1)}, u32[]{:S(2)}, u32[]{:S(2)}) collective-permute-start(bf16[48,1536]{1,0:T(8,128)(2,1)} %bitcast.32), channel_id=1, source_target_pairs={{0,16},{2,18},{4,20},{6,22},{8,24},{10,26},{12,28},{14,30},{16,0},... | collective-permute-start | bytes 442376 | tf_op jit(solution)/shard_map/ppermute | solution.py:472
  11.0 9.8 %collective-permute-done.7.refs_2_ = bf16[48,1536]{1,0:T(8,128)(2,1)S(1)} collective-permute-done((bf16[48,1536]{1,0:T(8,128)(2,1)}, bf16[48,1536]{1,0:T(8,128)(2,1)S(1)}, u32[]{:S(2)}, u32[]{:S(2)}) %collective-permute-start.7) | collective-permute-done | bytes 147488 | tf_op jit(solution)/shard_map/ppermute | solution.py:472
  22.2 1.6 collective-permute-start.15
  27.3 1.7 %collective-permute-done.15.refs_2_ = bf16[2,48,1536]{2,1,0:T(8,128)(2,1)S(1)} collective-permute-done((bf16[2,48,1536]{2,1,0:T(8,128)(2,1)S(1)}, bf16[2,48,1536]{2,1,0:T(8,128)(2,1)S(1)}, u32[]{:S(2)}, u32[]{:S(2)}) %collective-permute-start.15) | collective-permute-done | bytes 294944 | tf_op jit(solution)/shard_map/ppermute | solution.py:472
  29.6 4.9 %collective-permute-done.2.refs_2_ = bf16[2,48,1536]{2,1,0:T(8,128)(2,1)S(1)} collective-permute-done((bf16[2,48,1536]{2,1,0:T(8,128)(2,1)S(1)}, bf16[2,48,1536]{2,1,0:T(8,128)(2,1)S(1)}, u32[]{:S(2)}, u32[]{:S(2)}) %collective-permute-start.2) | collective-permute-done | bytes 294944 | tf_op jit(solution)/shard_map/ppermute | solution.py:472
  35.1 1.6 collective-permute-start.3
  40.1 1.5 collective-permute-start.13
  41.6 7.1 %collective-permute-done.3.refs_1_ = bf16[4,48,1536]{2,1,0:T(8,128)(2,1)S(1)} collective-permute-done((bf16[4,48,1536]{2,1,0:T(8,128)(2,1)S(1)}, bf16[4,48,1536]{2,1,0:T(8,128)(2,1)S(1)}, u32[]{:S(2)}, u32[]{:S(2)}) %collective-permute-start.3) | collective-permute-done | bytes 589856 | tf_op jit(solution)/shard_map/ppermute | solution.py:472
  49.9 2.5 %collective-permute-done.16.refs_2_ = bf16[4,48,1536]{2,1,0:T(8,128)(2,1)S(1)} collective-permute-done((bf16[4,48,1536]{2,1,0:T(8,128)(2,1)S(1)}, bf16[4,48,1536]{2,1,0:T(8,128)(2,1)S(1)}, u32[]{:S(2)}, u32[]{:S(2)}) %collective-permute-start.16) | collective-permute-done | bytes 589856 | tf_op jit(solution)/shard_map/ppermute | solution.py:472
  53.6 5.0 %collective-permute-done.13.refs_5_ = bf16[4,48,1536]{2,1,0:T(8,128)(2,1)S(1)} collective-permute-done((bf16[4,48,1536]{2,1,0:T(8,128)(2,1)S(1)}, bf16[4,48,1536]{2,1,0:T(8,128)(2,1)S(1)}, u32[]{:S(2)}, u32[]{:S(2)}) %collective-permute-start.13) | collective-permute-done | bytes 589856 | tf_op jit(solution)/shard_map/ppermute | solution.py:472
  61.8 5.8 %attend0.1 = (bf16[768,768]{1,0:T(8,128)(2,1)S(1)}, bf16[768,768]{1,0:T(8,128)(2,1)S(1)}, bf16[768,768]{1,0:T(8,128)(2,1)S(1)}, bf16[768,768]{1,0:T(8,128)(2,1)S...) custom-call(s32[12]{0:T(128)S(1)} %copy-done.13, ...), custom_call_target="tpu_custom_call" | custom-call | tf_op jit(solution)/shard_map/attend0/pallas_call | solution.py:379
  67.6 4.1 %feed0.1 = (bf16[768,1536]{1,0:T(8,128)(2,1)S(1)}, bf16[768,1536]{1,0:T(8,128)(2,1)S(1)}, bf16[384,768]{1,0:T(8,128)(2,1)S(1)}, f32[1,6912]{1,0:T(1,128)S(1)}, b...) custom-call(bf16[768,768]{1,0:T(8,128)(2,1)S(1)} %get-tuple-element.114.refs_8_.n2, f32[1,7680]{1,0:T(1,128)S(1)} %small.1, ...), custom_call_target="tpu_custom_call" | custom-call | flops 16499999744 | tf_op jit(solution)/shard_map/feed0/pallas_call | solution.py:379
  72.3 5.7 %attend1.1 = (bf16[768,768]{1,0:T(8,128)(2,1)S(1)}, bf16[768,768]{1,0:T(8,128)(2,1)S(1)}, bf16[768,768]{1,0:T(8,128)(2,1)S(1)}, bf16[768,768]{1,0:T(8,128)(2,1)S...) custom-call(s32[12]{0:T(128)S(1)} %copy-done.13, ...), custom_call_target="tpu_custom_call", output_to_operand_aliasing={{0}: (5, {}), {1}: (6, {}), {2}: (7, {}), {3}: (8, {}), {4}... | custom-call | tf_op jit(solution)/shard_map/attend1/pallas_call | solution.py:379
  78.0 3.3 %feed1.1 = (bf16[768,1536]{1,0:T(8,128)(2,1)S(1)}, bf16[768,1536]{1,0:T(8,128)(2,1)S(1)}, bf16[384,768]{1,0:T(8,128)(2,1)S(1)}, f32[1,6912]{1,0:T(1,128)S(1)}) custom-call(bf16[768,768]{1,0:T(8,128)(2,1)S(1)} %get-tuple-element.116.n2.refs_1_, f32[1,7680]{1,0:T(1,128)S(1)} %small.1, ...), custom_call_target="tpu_custom_call", output_to_operand_aliasing={{0}: (6, {}), {1}: (7, {})} | custom-call | tf_op jit(solution)/shard_map/feed1/pallas_call | solution.py:379
  81.3 1.6 collective-permute-start.26
  82.9 3.1 %grad_up.1 = (bf16[8,48,1536]{2,1,0:T(8,128)(2,1)S(1)}, bf16[8,48,1536]{2,1,0:T(8,128)(2,1)S(1)}) custom-call(s32[6]{0:T(128)S(1)} %stack.27.refs_0_.where.refs_3_, bf16[768,768]{1,0:T(8,128)(2,1)S(1)} %get-tuple-element.116.n2.refs_1_, bf16[768,1536]{1,0:T(8,128)(2,1)S(1)} %get-tuple-element.151.refs_2_), custom_call_target="tpu_custom_call" | custom-call | tf_op jit(solution)/shard_map/grad_up/pallas_call | solution.py:570
  86.0 2.0 %collective-permute-done.19.other = bf16[384,768]{1,0:T(8,128)(2,1)S(1)} collective-permute-done((bf16[384,768]{1,0:T(8,128)(2,1)S(1)}, bf16[384,768]{1,0:T(8,128)(2,1)S(1)}, u32[]{:S(2)}, u32[]{:S(2)}) %collective-permute-start.19) | collective-permute-done | bytes 589856 | tf_op jit(solution)/shard_map/ppermute | solution.py:472
  88.0 3.1 %grad_dn.1 = (bf16[8,48,1536]{2,1,0:T(8,128)(2,1)S(1)}, bf16[8,48,1536]{2,1,0:T(8,128)(2,1)S(1)}) custom-call(s32[6]{0:T(128)S(1)} %stack.27.refs_0_.where.refs_3_, bf16[768,768]{1,0:T(8,128)(2,1)S(1)} %bitcast.26, bf16[768,1536]{1,0:T(8,128)(2,1)S(1)} %get-tuple-element.123.refs_2_.act, bf16[8,48,1536]{2,1,0:T(8,128)(2,1)S(1)} %a_up.1.refs_1_.refs_3_), custom_call_target="tpu_custom_call" | custom-call | flops 16499999744 | tf_op jit(solution)/shard_map/grad_dn/pallas_call | solution.py:570
  94.8 7.9 %back0.1 = (bf16[768,768]{1,0:T(8,128)(2,1)S(1)}, bf16[768,2304]{1,0:T(8,128)(2,1)S(1)}, f32[1,6912]{1,0:T(1,128)S(1)}) custom-call(f32[768,768]{1,0:T(8,128)S(1)} %get-tuple-element.115.middle, bf16[384,768]{1,0:T(8,128)(2,1)S(1)} %get-tuple-element.126.own, bf16[384,768]{1,0:T(8,128)(2,1)S(1)} %collective-permute-done.19.other, ...), custom_call_target="tpu_custom_call" | custom-call | flops 16499999744 | tf_op jit(solution)/shard_map/back0/pallas_call | solution.py:379
  102.7 7.9 %back1.1 = (bf16[768,768]{1,0:T(8,128)(2,1)S(1)}, bf16[768,2304]{1,0:T(8,128)(2,1)S(1)}, f32[1,6912]{1,0:T(1,128)S(1)}) custom-call(f32[768,768]{1,0:T(8,128)S(1)} %get-tuple-element.115.middle, bf16[384,768]{1,0:T(8,128)(2,1)S(1)} %get-tuple-element.135.own, ...), custom_call_target="tpu_custom_call", output_to_operand_aliasing={{0}: (11, {}), {1}: (12, {})} | custom-call | flops 2200000000 | tf_op jit(solution)/shard_map/back1/pallas_call | solution.py:379
  110.6 2.0 %grad_out.1 = (bf16[8,48,384]{2,1,0:T(8,128)(2,1)S(1)}, bf16[8,48,384]{2,1,0:T(8,128)(2,1)S(1)}) custom-call(s32[6]{0:T(128)S(1)} %stack.27.refs_0_.where.refs_3_, bf16[768,768]{1,0:T(8,128)(2,1)S(1)} %get-tuple-element.157.refs_1_.gp, bf16[768,384]{1,0:T(8,128)(2,1)S(1)} %get-tuple-element.158.refs_2_), custom_call_target="tpu_custom_call" | custom-call | tf_op jit(solution)/shard_map/grad_out/pallas_call | solution.py:570
  113.7 1.6 collective-permute-start.32
  116.4 3.7 %rows0.1 = (bf16[768,768]{1,0:T(8,128)(2,1)}, f32[1,6912]{1,0:T(1,128)S(1)}) custom-call(s32[6]{0:T(128)S(1)} %stack.27.refs_0_.where.refs_3_, bf16[768,2304]{1,0:T(8,128)(2,1)S(1)} %get-tuple-element.144.refs_2_.gqkv, bf16[2,768,1536]{2,1,0:T(8,128)(2,1)S(1)} %get-tuple-element.106.refs_0_.w, bf16[768,768]{1,0:T(8,128)(2,1)S(1)} %bitcast.22, ...), custom_call_target="tpu_custom_call" | custom-call | tf_op jit(solution)/shard_map/rows0/pallas_call | solution.py:379
  120.0 3.7 %rows1.1 = (bf16[768,768]{1,0:T(8,128)(2,1)}, f32[1,6912]{1,0:T(1,128)S(1)}) custom-call(s32[6]{0:T(128)S(1)} %stack.27.refs_0_.where.refs_3_, bf16[768,2304]{1,0:T(8,128)(2,1)S(1)} %get-tuple-element.144.refs_2_.gqkv, bf16[2,768,1536]{2,1,0:T(8,128)(2,1)S(1)} %get-tuple-element.106.refs_0_.w, ...), custom_call_target="tpu_custom_call", output_to_operand_aliasing={{0}: (8, {})} | custom-call | tf_op jit(solution)/shard_map/rows1/pallas_call | solution.py:379
  123.7 2.8 %grad_qkv.1 = (bf16[8,48,1152]{2,1,0:T(8,128)(2,1)S(1)}, bf16[8,48,1152]{2,1,0:T(8,128)(2,1)S(1)}) custom-call(s32[6]{0:T(128)S(1)} %stack.27.refs_0_.where.refs_3_, bf16[768,768]{1,0:T(8,128)(2,1)S(1)} %get-tuple-element.134.refs_1_, bf16[768,2304]{1,0:T(8,128)(2,1)S(1)} %get-tuple-element.144.refs_2_.gqkv), custom_call_target="tpu_custom_call" | custom-call | flops 2200000000 | tf_op jit(solution)/shard_map/grad_qkv/pallas_call | solution.py:570
  131.7 2.8 %collective-permute-done.35.refs_2_ = bf16[240,384]{1,0:T(8,128)(2,1)S(1)} collective-permute-done((bf16[240,384]{1,0:T(8,128)(2,1)S(1)}, bf16[240,384]{1,0:T(8,128)(2,1)S(1)}, u32[]{:S(2)}, u32[]{:S(2)}) %collective-permute-start.35) | collective-permute-done | bytes 184352 | tf_op jit(solution)/shard_map/ppermute | solution.py:472
  135.2 3.9 %collective-permute-start.36 = (bf16[144,384]{1,0:T(8,128)(2,1)S(1)}, bf16[144,384]{1,0:T(8,128)(2,1)S(1)}, u32[]{:S(2)}, u32[]{:S(2)}) collective-permute-start(bf16[144,384]{1,0:T(8,128)(2,1)S(1)} %get-tuple-element.175), channel_id=1, source_target_pairs={{0,16},{2,18},{4,20},{6,22},{8,24},{10,26},{12,28},{14,30},{16,0},... | collective-permute-start | bytes 331784 | tf_op jit(solution)/shard_map/ppermute | solution.py:472
  144.0 2.0 %collective-permute-start.39 = (bf16[48,1536]{1,0:T(8,128)(2,1)S(1)}, bf16[48,1536]{1,0:T(8,128)(2,1)S(1)}, u32[]{:S(2)}, u32[]{:S(2)}) collective-permute-start(bf16[48,1536]{1,0:T(8,128)(2,1)S(1)} %get-tuple-element.189.refs_3_), channel_id=1, source_target_pairs={{0,16},{2,18},{4,20},{6,22},{8,24},{10,26},{12,28},{14,30},{16,0},... | collective-permute-start | bytes 442376 | tf_op jit(solution)/shard_map/ppermute | solution.py:472
  149.2 3.1 %collective-permute-done.24.refs_2_ = bf16[2,48,1536]{2,1,0:T(8,128)(2,1)S(1)} collective-permute-done((bf16[2,48,1536]{2,1,0:T(8,128)(2,1)S(1)}, bf16[2,48,1536]{2,1,0:T(8,128)(2,1)S(1)}, u32[]{:S(2)}, u32[]{:S(2)}) %collective-permute-start.24) | collective-permute-done | bytes 294944 | tf_op jit(solution)/shard_map/ppermute | solution.py:472
  155.0 4.1 %collective-permute-done.29.refs_2_ = bf16[2,48,1152]{2,1,0:T(8,128)(2,1)S(1)} collective-permute-done((bf16[2,48,1152]{2,1,0:T(8,128)(2,1)S(1)}, bf16[2,48,1152]{2,1,0:T(8,128)(2,1)S(1)}, u32[]{:S(2)}, u32[]{:S(2)}) %collective-permute-start.29) | collective-permute-done | bytes 221216 | tf_op jit(solution)/shard_map/ppermute | solution.py:472
  (119 shorter events, 48.3 us)
Async XLA Ops:
  0.7 7.2 %collective-permute-start = (f32[2,384]{1,0:T(2,128)}, f32[2,384]{1,0:T(2,128)S(1)}, u32[]{:S(2)}, u32[]{:S(2)}) collective-permute-start(f32[2,384]{1,0:T(2,128)} %refs_1_.2), channel_id=1, source_target_pairs={{0,1},{1,0},{2,3},{3,2},{4,5},{5,4},{6,7},{7,6},{8,9},{9,8},{10,11... | collective-permute-start | bytes 9224 | tf_op jit(solution)/shard_map/ppermute | solution.py:472
  3.7 17.1 %collective-permute-start.7 = (bf16[48,1536]{1,0:T(8,128)(2,1)}, bf16[48,1536]{1,0:T(8,128)(2,1)S(1)}, u32[]{:S(2)}, u32[]{:S(2)}) collective-permute-start(bf16[48,1536]{1,0:T(8,128)(2,1)} %refs_1_.3), channel_id=1, source_target_pairs={{0,16},{2,18},{4,20},{6,22},{8,24},{10,26},{12,28},{14,30},{16,0},... | collective-permute-start | bytes 442376 | tf_op jit(solution)/shard_map/ppermute | solution.py:472
  7.9 16.0 %collective-permute-start.1 = (bf16[48,1536]{1,0:T(8,128)(2,1)S(1)}, bf16[48,1536]{1,0:T(8,128)(2,1)S(1)}, u32[]{:S(2)}, u32[]{:S(2)}) collective-permute-start(bf16[48,1536]{1,0:T(8,128)(2,1)S(1)} %pad_maximum_fusion.refs_1_), channel_id=1, source_target_pairs={{0,16},{2,18},{4,20},{6,22},{8,24},{10,26},{12,28},{14,30},{16,0},... | collective-permute-start | bytes 442376 | tf_op jit(solution)/shard_map/ppermute | solution.py:472
  8.6 17.4 %collective-permute-start.11 = (bf16[48,1536]{1,0:T(8,128)(2,1)}, bf16[48,1536]{1,0:T(8,128)(2,1)S(1)}, u32[]{:S(2)}, u32[]{:S(2)}) collective-permute-start(bf16[48,1536]{1,0:T(8,128)(2,1)} %bitcast.32), channel_id=1, source_target_pairs={{0,16},{2,18},{4,20},{6,22},{8,24},{10,26},{12,28},{14,30},{16,0},... | collective-permute-start | bytes 442376 | tf_op jit(solution)/shard_map/ppermute | solution.py:472
  22.2 6.8 %collective-permute-start.15 = (bf16[2,48,1536]{2,1,0:T(8,128)(2,1)S(1)}, bf16[2,48,1536]{2,1,0:T(8,128)(2,1)S(1)}, u32[]{:S(2)}, u32[]{:S(2)}) collective-permute-start(bf16[2,48,1536]{2,1,0:T(8,128)(2,1)S(1)} %p_up.1.refs_1_), channel_id=1, source_target_pairs={{0,4},{2,6},{4,0},{6,2},{8,12},{10,14},{12,8},{14,10},{16,20},{18,... | collective-permute-start | bytes 884744 | tf_op jit(solution)/shard_map/ppermute | solution.py:472
  24.5 10.0 %collective-permute-start.2 = (bf16[2,48,1536]{2,1,0:T(8,128)(2,1)S(1)}, bf16[2,48,1536]{2,1,0:T(8,128)(2,1)S(1)}, u32[]{:S(2)}, u32[]{:S(2)}) collective-permute-start(bf16[2,48,1536]{2,1,0:T(8,128)(2,1)S(1)} %p_att.1.refs_1_), channel_id=1, source_target_pairs={{0,8},{2,10},{4,12},{6,14},{8,0},{10,2},{12,4},{14,6},{16,24},{18,... | collective-permute-start | bytes 884744 | tf_op jit(solution)/shard_map/ppermute | solution.py:472
  26.6 12.0 %collective-permute-start.12 = (bf16[2,48,1536]{2,1,0:T(8,128)(2,1)S(1)}, bf16[2,48,1536]{2,1,0:T(8,128)(2,1)S(1)}, u32[]{:S(2)}, u32[]{:S(2)}) collective-permute-start(bf16[2,48,1536]{2,1,0:T(8,128)(2,1)S(1)} %p_dn.1.refs_1_), channel_id=1, source_target_pairs={{0,8},{2,10},{4,12},{6,14},{8,0},{10,2},{12,4},{14,6},{16,24},{18,... | collective-permute-start | bytes 884744 | tf_op jit(solution)/shard_map/ppermute | solution.py:472
  35.1 13.6 %collective-permute-start.3 = (bf16[4,48,1536]{2,1,0:T(8,128)(2,1)S(1)}, bf16[4,48,1536]{2,1,0:T(8,128)(2,1)S(1)}, u32[]{:S(2)}, u32[]{:S(2)}) collective-permute-start(bf16[4,48,1536]{2,1,0:T(8,128)(2,1)S(1)} %a_att.1.refs_0_), channel_id=1, source_target_pairs={{0,4},{2,6},{4,0},{6,2},{8,12},{10,14},{12,8},{14,10},{16,20},{18,... | collective-permute-start | bytes 1769480 | tf_op jit(solution)/shard_map/ppermute | solution.py:472
  36.6 13.2 %collective-permute-start.6 = (bf16[4,48,1536]{2,1,0:T(8,128)(2,1)S(1)}, bf16[4,48,1536]{2,1,0:T(8,128)(2,1)S(1)}, u32[]{:S(2)}, u32[]{:S(2)}) collective-permute-start(bf16[4,48,1536]{2,1,0:T(8,128)(2,1)S(1)} %a_att.1.refs_0_), channel_id=1, source_target_pairs={{0,1},{1,0},{2,3},{3,2},{4,5},{5,4},{6,7},{7,6},{8,9},{9,8},{10,11... | collective-permute-start | bytes 1769480 | tf_op jit(solution)/shard_map/ppermute | solution.py:472
  39.3 13.1 %collective-permute-start.16 = (bf16[4,48,1536]{2,1,0:T(8,128)(2,1)S(1)}, bf16[4,48,1536]{2,1,0:T(8,128)(2,1)S(1)}, u32[]{:S(2)}, u32[]{:S(2)}) collective-permute-start(bf16[4,48,1536]{2,1,0:T(8,128)(2,1)S(1)} %px_up.1.refs_1_), channel_id=1, source_target_pairs={{0,8},{2,10},{4,12},{6,14},{8,0},{10,2},{12,4},{14,6},{16,24},{18,... | collective-permute-start | bytes 1769480 | tf_op jit(solution)/shard_map/ppermute | solution.py:472
  40.1 13.0 %collective-permute-start.4 = (bf16[4,48,1536]{2,1,0:T(8,128)(2,1)S(1)}, bf16[4,48,1536]{2,1,0:T(8,128)(2,1)S(1)}, u32[]{:S(2)}, u32[]{:S(2)}) collective-permute-start(bf16[4,48,1536]{2,1,0:T(8,128)(2,1)S(1)} %a_att.1.refs_0_), channel_id=1, source_target_pairs={{0,2},{2,0},{4,6},{6,4},{8,10},{10,8},{12,14},{14,12},{16,18},{18,... | collective-permute-start | bytes 1769480 | tf_op jit(solution)/shard_map/ppermute | solution.py:472
  40.1 18.5 %collective-permute-start.13 = (bf16[4,48,1536]{2,1,0:T(8,128)(2,1)S(1)}, bf16[4,48,1536]{2,1,0:T(8,128)(2,1)S(1)}, u32[]{:S(2)}, u32[]{:S(2)}) collective-permute-start(bf16[4,48,1536]{2,1,0:T(8,128)(2,1)S(1)} %a_dn.1.refs_4_), channel_id=1, source_target_pairs={{0,4},{2,6},{4,0},{6,2},{8,12},{10,14},{12,8},{14,10},{16,20},{18,... | collective-permute-start | bytes 1769480 | tf_op jit(solution)/shard_map/ppermute | solution.py:472
  48.7 11.1 %collective-permute-start.8 = (bf16[4,48,1536]{2,1,0:T(8,128)(2,1)S(1)}, bf16[4,48,1536]{2,1,0:T(8,128)(2,1)S(1)}, u32[]{:S(2)}, u32[]{:S(2)}) collective-permute-start(bf16[4,48,1536]{2,1,0:T(8,128)(2,1)S(1)} %collective-permute-done.3.refs_1_), channel_id=1, source_target_pairs={{0,1},{1,0},{2,3},{3,2},{4,5},{5,4},{6,7},{7,6},{8,9},{9,8},{10,11... | collective-permute-start | bytes 1769480 | tf_op jit(solution)/shard_map/ppermute | solution.py:472
  49.9 9.9 %collective-permute-start.9 = (bf16[4,48,1536]{2,1,0:T(8,128)(2,1)S(1)}, bf16[4,48,1536]{2,1,0:T(8,128)(2,1)S(1)}, u32[]{:S(2)}, u32[]{:S(2)}) collective-permute-start(bf16[4,48,1536]{2,1,0:T(8,128)(2,1)S(1)} %collective-permute-done.6.refs_4_), channel_id=1, source_target_pairs={{0,2},{2,0},{4,6},{6,4},{8,10},{10,8},{12,14},{14,12},{16,18},{18,... | collective-permute-start | bytes 1769480 | tf_op jit(solution)/shard_map/ppermute | solution.py:472
  53.0 14.6 %collective-permute-start.17 = (bf16[8,48,1536]{2,1,0:T(8,128)(2,1)S(1)}, bf16[8,48,1536]{2,1,0:T(8,128)(2,1)S(1)}, u32[]{:S(2)}, u32[]{:S(2)}) collective-permute-start(bf16[8,48,1536]{2,1,0:T(8,128)(2,1)S(1)} %a_up.1.refs_1_.refs_3_), channel_id=1, source_target_pairs={{0,2},{2,0},{4,6},{6,4},{8,10},{10,8},{12,14},{14,12},{16,18},{18,... | collective-permute-start | bytes 3538952 | tf_op jit(solution)/shard_map/ppermute | solution.py:472
  53.1 7.8 %collective-permute-start.5 = (bf16[4,48,1536]{2,1,0:T(8,128)(2,1)S(1)}, bf16[4,48,1536]{2,1,0:T(8,128)(2,1)S(1)}, u32[]{:S(2)}, u32[]{:S(2)}) collective-permute-start(bf16[4,48,1536]{2,1,0:T(8,128)(2,1)S(1)} %collective-permute-done.3.refs_1_), channel_id=1, source_target_pairs={{0,2},{2,0},{4,6},{6,4},{8,10},{10,8},{12,14},{14,12},{16,18},{18,... | collective-permute-start | bytes 1769480 | tf_op jit(solution)/shard_map/ppermute | solution.py:472
  59.8 7.8 %collective-permute-start.18 = (bf16[4,48,1536]{2,1,0:T(8,128)(2,1)S(1)}, bf16[4,48,1536]{2,1,0:T(8,128)(2,1)S(1)}, u32[]{:S(2)}, u32[]{:S(2)}) collective-permute-start(bf16[4,48,1536]{2,1,0:T(8,128)(2,1)S(1)} %a_dn.1.refs_4_), channel_id=1, source_target_pairs={{0,2},{2,0},{4,6},{6,4},{8,10},{10,8},{12,14},{14,12},{16,18},{18,... | collective-permute-start | bytes 1769480 | tf_op jit(solution)/shard_map/ppermute | solution.py:472
  71.8 16.2 %collective-permute-start.19 = (bf16[384,768]{1,0:T(8,128)(2,1)S(1)}, bf16[384,768]{1,0:T(8,128)(2,1)S(1)}, u32[]{:S(2)}, u32[]{:S(2)}) collective-permute-start(bf16[384,768]{1,0:T(8,128)(2,1)S(1)} %get-tuple-element.126.own), channel_id=1, source_target_pairs={{0,1},{1,0},{2,3},{3,2},{4,5},{5,4},{6,7},{7,6},{8,9},{9,8},{10,11... | collective-permute-start | bytes 1769480 | tf_op jit(solution)/shard_map/ppermute | solution.py:472
  81.3 21.4 %collective-permute-start.26 = (bf16[384,768]{1,0:T(8,128)(2,1)S(1)}, bf16[384,768]{1,0:T(8,128)(2,1)S(1)}, u32[]{:S(2)}, u32[]{:S(2)}) collective-permute-start(bf16[384,768]{1,0:T(8,128)(2,1)S(1)} %get-tuple-element.135.own), channel_id=1, source_target_pairs={{0,1},{1,0},{2,3},{3,2},{4,5},{5,4},{6,7},{7,6},{8,9},{9,8},{10,11... | collective-permute-start | bytes 1769480 | tf_op jit(solution)/shard_map/ppermute | solution.py:472
  92.4 20.7 %collective-permute-start.31 = (bf16[4,48,1536]{2,1,0:T(8,128)(2,1)S(1)}, bf16[4,48,1536]{2,1,0:T(8,128)(2,1)S(1)}, u32[]{:S(2)}, u32[]{:S(2)}) collective-permute-start(bf16[4,48,1536]{2,1,0:T(8,128)(2,1)S(1)} %get-tuple-element.156), channel_id=1, source_target_pairs={{0,4},{2,6},{4,0},{6,2},{8,12},{10,14},{12,8},{14,10},{16,20},{18,... | collective-permute-start | bytes 1769480 | tf_op jit(solution)/shard_map/ppermute | solution.py:472
  112.6 14.4 %collective-permute-start.33 = (bf16[8,48,384]{2,1,0:T(8,128)(2,1)S(1)}, bf16[8,48,384]{2,1,0:T(8,128)(2,1)S(1)}, u32[]{:S(2)}, u32[]{:S(2)}) collective-permute-start(bf16[8,48,384]{2,1,0:T(8,128)(2,1)S(1)} %get-tuple-element.169.refs_3_), channel_id=1, source_target_pairs={{0,2},{2,0},{4,6},{6,4},{8,10},{10,8},{12,14},{14,12},{16,18},{18,... | collective-permute-start | bytes 884744 | tf_op jit(solution)/shard_map/ppermute | solution.py:472
  113.7 13.4 %collective-permute-start.32 = (bf16[2,48,1536]{2,1,0:T(8,128)(2,1)S(1)}, bf16[2,48,1536]{2,1,0:T(8,128)(2,1)S(1)}, u32[]{:S(2)}, u32[]{:S(2)}) collective-permute-start(bf16[2,48,1536]{2,1,0:T(8,128)(2,1)S(1)} %get-tuple-element.161), channel_id=1, source_target_pairs={{0,8},{2,10},{4,12},{6,14},{8,0},{10,2},{12,4},{14,6},{16,24},{18,... | collective-permute-start | bytes 884744 | tf_op jit(solution)/shard_map/ppermute | solution.py:472
  115.2 23.9 %collective-permute-start.21 = (bf16[4,48,1536]{2,1,0:T(8,128)(2,1)S(1)}, bf16[4,48,1536]{2,1,0:T(8,128)(2,1)S(1)}, u32[]{:S(2)}, u32[]{:S(2)}) collective-permute-start(bf16[4,48,1536]{2,1,0:T(8,128)(2,1)S(1)} %get-tuple-element.128.refs_0_), channel_id=1, source_target_pairs={{0,4},{2,6},{4,0},{6,2},{8,12},{10,14},{12,8},{14,10},{16,20},{18,... | collective-permute-start | bytes 1769480 | tf_op jit(solution)/shard_map/ppermute | solution.py:472
  129.5 18.8 %collective-permute-start.23 = (bf16[384,768]{1,0:T(8,128)(2,1)S(1)}, bf16[384,768]{1,0:T(8,128)(2,1)S(1)}, u32[]{:S(2)}, u32[]{:S(2)}) collective-permute-start(bf16[384,768]{1,0:T(8,128)(2,1)S(1)} %down0.1.own), channel_id=1, source_target_pairs={{0,1},{1,0},{2,3},{3,2},{4,5},{5,4},{6,7},{7,6},{8,9},{9,8},{10,11... | collective-permute-start | bytes 1769480 | tf_op jit(solution)/shard_map/ppermute | solution.py:472
  130.8 16.0 %collective-permute-start.28 = (bf16[4,48,1152]{2,1,0:T(8,128)(2,1)S(1)}, bf16[4,48,1152]{2,1,0:T(8,128)(2,1)S(1)}, u32[]{:S(2)}, u32[]{:S(2)}) collective-permute-start(bf16[4,48,1152]{2,1,0:T(8,128)(2,1)S(1)} %get-tuple-element.148), channel_id=1, source_target_pairs={{0,4},{2,6},{4,0},{6,2},{8,12},{10,14},{12,8},{14,10},{16,20},{18,... | collective-permute-start | bytes 1327112 | tf_op jit(solution)/shard_map/ppermute | solution.py:472
  135.2 8.8 %collective-permute-start.36 = (bf16[144,384]{1,0:T(8,128)(2,1)S(1)}, bf16[144,384]{1,0:T(8,128)(2,1)S(1)}, u32[]{:S(2)}, u32[]{:S(2)}) collective-permute-start(bf16[144,384]{1,0:T(8,128)(2,1)S(1)} %get-tuple-element.175), channel_id=1, source_target_pairs={{0,16},{2,18},{4,20},{6,22},{8,24},{10,26},{12,28},{14,30},{16,0},... | collective-permute-start | bytes 331784 | tf_op jit(solution)/shard_map/ppermute | solution.py:472
  139.7 12.6 %collective-permute-start.24 = (bf16[2,48,1536]{2,1,0:T(8,128)(2,1)S(1)}, bf16[2,48,1536]{2,1,0:T(8,128)(2,1)S(1)}, u32[]{:S(2)}, u32[]{:S(2)}) collective-permute-start(bf16[2,48,1536]{2,1,0:T(8,128)(2,1)S(1)} %get-tuple-element.131), channel_id=1, source_target_pairs={{0,8},{2,10},{4,12},{6,14},{8,0},{10,2},{12,4},{14,6},{16,24},{18,... | collective-permute-start | bytes 884744 | tf_op jit(solution)/shard_map/ppermute | solution.py:472
  141.5 22.1 %collective-permute-start.22 = (bf16[384,768]{1,0:T(8,128)(2,1)S(1)}, bf16[384,768]{1,0:T(8,128)(2,1)S(1)}, u32[]{:S(2)}, u32[]{:S(2)}) collective-permute-start(bf16[384,768]{1,0:T(8,128)(2,1)S(1)} %down1.1.own), channel_id=1, source_target_pairs={{0,1},{1,0},{2,3},{3,2},{4,5},{5,4},{6,7},{7,6},{8,9},{9,8},{10,11... | collective-permute-start | bytes 1769480 | tf_op jit(solution)/shard_map/ppermute | solution.py:472
  144.0 9.6 %collective-permute-start.39 = (bf16[48,1536]{1,0:T(8,128)(2,1)S(1)}, bf16[48,1536]{1,0:T(8,128)(2,1)S(1)}, u32[]{:S(2)}, u32[]{:S(2)}) collective-permute-start(bf16[48,1536]{1,0:T(8,128)(2,1)S(1)} %get-tuple-element.189.refs_3_), channel_id=1, source_target_pairs={{0,16},{2,18},{4,20},{6,22},{8,24},{10,26},{12,28},{14,30},{16,0},... | collective-permute-start | bytes 442376 | tf_op jit(solution)/shard_map/ppermute | solution.py:472
  146.8 7.6 %collective-permute-start.37 = (bf16[96,384]{1,0:T(8,128)(2,1)S(1)}, bf16[96,384]{1,0:T(8,128)(2,1)S(1)}, u32[]{:S(2)}, u32[]{:S(2)}) collective-permute-start(bf16[96,384]{1,0:T(8,128)(2,1)S(1)} %get-tuple-element.178), channel_id=1, source_target_pairs={{0,4},{2,6},{4,0},{6,2},{8,12},{10,14},{12,8},{14,10},{16,20},{18,... | collective-permute-start | bytes 221192 | tf_op jit(solution)/shard_map/ppermute | solution.py:472
  148.3 10.8 %collective-permute-start.29 = (bf16[2,48,1152]{2,1,0:T(8,128)(2,1)S(1)}, bf16[2,48,1152]{2,1,0:T(8,128)(2,1)S(1)}, u32[]{:S(2)}, u32[]{:S(2)}) collective-permute-start(bf16[2,48,1152]{2,1,0:T(8,128)(2,1)S(1)} %get-tuple-element.150), channel_id=1, source_target_pairs={{0,8},{2,10},{4,12},{6,14},{8,0},{10,2},{12,4},{14,6},{16,24},{18,... | collective-permute-start | bytes 663560 | tf_op jit(solution)/shard_map/ppermute | solution.py:472
  152.9 7.9 %collective-permute-start.25 = (bf16[48,1536]{1,0:T(8,128)(2,1)S(1)}, bf16[48,1536]{1,0:T(8,128)(2,1)S(1)}, u32[]{:S(2)}, u32[]{:S(2)}) collective-permute-start(bf16[48,1536]{1,0:T(8,128)(2,1)S(1)} %get-tuple-element.133), channel_id=1, source_target_pairs={{0,16},{2,18},{4,20},{6,22},{8,24},{10,26},{12,28},{14,30},{16,0},... | collective-permute-start | bytes 442376 | tf_op jit(solution)/shard_map/ppermute | solution.py:472
  (22 other events, 278.5 us)
where the time goes:
time: 167 us
  Pallas kernels  72.6 us (43%)
  waiting for transfers between devices  53.6 us (32%)
  starting transfers between devices  35.9 us (21%)
  local copies, waits for them, and re-layouts  2.84 us (2%)
    ppermute x40, waiting for transfers between devices, move(): return made(name, lax.ppermute(after(v, *need(name)), axis, pairs))  53.6 us
    pallas_call x12, Pallas kernels, call(): pl.pallas_call(functools.partial(kernel, len(aliases) + len(deps)), grid=...  46.4 us
    ppermute x40, starting transfers between devices, move(): return made(name, lax.ppermute(after(v, *need(name)), axis, pairs))  35.9 us
    pallas_call x24, Pallas kernels, simple(): pl.pallas_call(body, grid=(1,), in_specs=specs, out_specs=[whole_spec(sha...  15.4 us
    pallas_call x4, Pallas kernels, weight_grad(): pl.pallas_call(body, grid=(steps,), in_specs=[SMEM_SPEC, pl.BlockSpec((ro...  10.9 us
  transfers between devices with their start and end apart: 40, of which 21 were waited for; matrix products, arithmetic and copies ran while one was open for 1% of the time, Pallas kernels for 41%

commit v1 on v0

--- a/solution.py
+++ b/solution.py
@@ -292,18 +292,12 @@
             vc = two_heads(v[r, lanes], low)
             pr = probs[t * pairs + p]
             gprob = mm(g2, vc, NT)
-            prod = pr * gprob
-            tot = jnp.concatenate(
-                [
-                    jnp.broadcast_to(
-                        jnp.sum(prod[:, i * PAIR : (i + 1) * PAIR], axis=-1, keepdims=True),
-                        (PAIR, PAIR),
-                    )
-                    for i in range(2)
-                ],
-                axis=1,
-            )
-            gs = (pr * (gprob - tot)).astype(BF)
+            halves = []
+            for i in range(2):
+                p_h, g_h = (a[:, i * PAIR : (i + 1) * PAIR] for a in (pr, gprob))
+                row_sum = jnp.sum(p_h * g_h, axis=-1, keepdims=True)
+                halves.append((p_h * (g_h - row_sum)).astype(BF))
+            gs = jnp.concatenate(halves, axis=1)
             gq = mm(gs, kc) * (HD**-0.5)
             gk = mm(gs, q2, TN)
             gv = mm(pr.astype(BF), g2, TN)

time: 167 us -> 167 us (level)
  no operation moved by 1% of the time
where the time goes in v1:
time: 167 us
  Pallas kernels  72.6 us (43%)
  waiting for transfers between devices  53.6 us (32%)
  starting transfers between devices  35.9 us (21%)
  local copies, waits for them, and re-layouts  2.84 us (2%)
    ppermute x40, waiting for transfers between devices, move(): return made(name, lax.ppermute(after(v, *need(name)), axis, pairs))  53.6 us
    pallas_call x12, Pallas kernels, call(): pl.pallas_call(functools.partial(kernel, len(aliases) + len(deps)), grid=...  46.4 us
    ppermute x40, starting transfers between devices, move(): return made(name, lax.ppermute(after(v, *need(name)), axis, pairs))  35.9 us
    pallas_call x24, Pallas kernels, simple(): pl.pallas_call(body, grid=(1,), in_specs=specs, out_specs=[whole_spec(sha...  15.4 us
    pallas_call x4, Pallas kernels, weight_grad(): pl.pallas_call(body, grid=(steps,), in_specs=[SMEM_SPEC, pl.BlockSpec((ro...  10.9 us
  transfers between devices with their start and end apart: 40, of which 21 were waited for; matrix products, arithmetic and copies ran while one was open for 1% of the time, Pallas kernels for 41%

profile of v1, /device:TPU:0, one launch (start us, length us, event | category | flops | bytes accessed | tf_op | source)
XLA Modules:
  0.0 166.8 jit_solution(17903376427838661845)
XLA Ops:
  0.7 3.0 %collective-permute-start = (f32[2,384]{1,0:T(2,128)}, f32[2,384]{1,0:T(2,128)S(1)}, u32[]{:S(2)}, u32[]{:S(2)}) collective-permute-start(f32[2,384]{1,0:T(2,128)} %refs_1_.2), channel_id=1, source_target_pairs={{0,1},{1,0},{2,3},{3,2},{4,5},{5,4},{6,7},{7,6},{8,9},{9,8},{10,11... | collective-permute-start | bytes 9224 | tf_op jit(solution)/shard_map/ppermute | solution.py:466
  3.7 2.6 %collective-permute-start.7 = (bf16[48,1536]{1,0:T(8,128)(2,1)}, bf16[48,1536]{1,0:T(8,128)(2,1)S(1)}, u32[]{:S(2)}, u32[]{:S(2)}) collective-permute-start(bf16[48,1536]{1,0:T(8,128)(2,1)} %refs_1_.3), channel_id=1, source_target_pairs={{0,16},{2,18},{4,20},{6,22},{8,24},{10,26},{12,28},{14,30},{16,0},... | collective-permute-start | bytes 442376 | tf_op jit(solution)/shard_map/ppermute | solution.py:466
  8.6 2.3 %collective-permute-start.11 = (bf16[48,1536]{1,0:T(8,128)(2,1)}, bf16[48,1536]{1,0:T(8,128)(2,1)S(1)}, u32[]{:S(2)}, u32[]{:S(2)}) collective-permute-start(bf16[48,1536]{1,0:T(8,128)(2,1)} %bitcast.32), channel_id=1, source_target_pairs={{0,16},{2,18},{4,20},{6,22},{8,24},{10,26},{12,28},{14,30},{16,0},... | collective-permute-start | bytes 442376 | tf_op jit(solution)/shard_map/ppermute | solution.py:466
  11.0 9.8 %collective-permute-done.7.refs_2_ = bf16[48,1536]{1,0:T(8,128)(2,1)S(1)} collective-permute-done((bf16[48,1536]{1,0:T(8,128)(2,1)}, bf16[48,1536]{1,0:T(8,128)(2,1)S(1)}, u32[]{:S(2)}, u32[]{:S(2)}) %collective-permute-start.7) | collective-permute-done | bytes 147488 | tf_op jit(solution)/shard_map/ppermute | solution.py:466
  22.2 1.6 collective-permute-start.15
  27.3 1.7 %collective-permute-done.15.refs_2_ = bf16[2,48,1536]{2,1,0:T(8,128)(2,1)S(1)} collective-permute-done((bf16[2,48,1536]{2,1,0:T(8,128)(2,1)S(1)}, bf16[2,48,1536]{2,1,0:T(8,128)(2,1)S(1)}, u32[]{:S(2)}, u32[]{:S(2)}) %collective-permute-start.15) | collective-permute-done | bytes 294944 | tf_op jit(solution)/shard_map/ppermute | solution.py:466
  29.6 4.9 %collective-permute-done.2.refs_2_ = bf16[2,48,1536]{2,1,0:T(8,128)(2,1)S(1)} collective-permute-done((bf16[2,48,1536]{2,1,0:T(8,128)(2,1)S(1)}, bf16[2,48,1536]{2,1,0:T(8,128)(2,1)S(1)}, u32[]{:S(2)}, u32[]{:S(2)}) %collective-permute-start.2) | collective-permute-done | bytes 294944 | tf_op jit(solution)/shard_map/ppermute | solution.py:466
  35.1 1.6 collective-permute-start.3
  40.1 1.5 collective-permute-start.13
  41.6 7.1 %collective-permute-done.3.refs_1_ = bf16[4,48,1536]{2,1,0:T(8,128)(2,1)S(1)} collective-permute-done((bf16[4,48,1536]{2,1,0:T(8,128)(2,1)S(1)}, bf16[4,48,1536]{2,1,0:T(8,128)(2,1)S(1)}, u32[]{:S(2)}, u32[]{:S(2)}) %collective-permute-start.3) | collective-permute-done | bytes 589856 | tf_op jit(solution)/shard_map/ppermute | solution.py:466
  49.9 2.5 %collective-permute-done.16.refs_2_ = bf16[4,48,1536]{2,1,0:T(8,128)(2,1)S(1)} collective-permute-done((bf16[4,48,1536]{2,1,0:T(8,128)(2,1)S(1)}, bf16[4,48,1536]{2,1,0:T(8,128)(2,1)S(1)}, u32[]{:S(2)}, u32[]{:S(2)}) %collective-permute-start.16) | collective-permute-done | bytes 589856 | tf_op jit(solution)/shard_map/ppermute | solution.py:466
  53.6 5.0 %collective-permute-done.13.refs_5_ = bf16[4,48,1536]{2,1,0:T(8,128)(2,1)S(1)} collective-permute-done((bf16[4,48,1536]{2,1,0:T(8,128)(2,1)S(1)}, bf16[4,48,1536]{2,1,0:T(8,128)(2,1)S(1)}, u32[]{:S(2)}, u32[]{:S(2)}) %collective-permute-start.13) | collective-permute-done | bytes 589856 | tf_op jit(solution)/shard_map/ppermute | solution.py:466
  61.8 5.8 %attend0.1 = (bf16[768,768]{1,0:T(8,128)(2,1)S(1)}, bf16[768,768]{1,0:T(8,128)(2,1)S(1)}, bf16[768,768]{1,0:T(8,128)(2,1)S(1)}, bf16[768,768]{1,0:T(8,128)(2,1)S...) custom-call(s32[12]{0:T(128)S(1)} %copy-done.13, ...), custom_call_target="tpu_custom_call" | custom-call | tf_op jit(solution)/shard_map/attend0/pallas_call | solution.py:373
  67.6 4.1 %feed0.1 = (bf16[768,1536]{1,0:T(8,128)(2,1)S(1)}, bf16[768,1536]{1,0:T(8,128)(2,1)S(1)}, bf16[384,768]{1,0:T(8,128)(2,1)S(1)}, f32[1,6912]{1,0:T(1,128)S(1)}, b...) custom-call(bf16[768,768]{1,0:T(8,128)(2,1)S(1)} %get-tuple-element.114.refs_8_.n2, f32[1,7680]{1,0:T(1,128)S(1)} %small.1, ...), custom_call_target="tpu_custom_call" | custom-call | flops 16499999744 | tf_op jit(solution)/shard_map/feed0/pallas_call | solution.py:373
  72.3 5.7 %attend1.1 = (bf16[768,768]{1,0:T(8,128)(2,1)S(1)}, bf16[768,768]{1,0:T(8,128)(2,1)S(1)}, bf16[768,768]{1,0:T(8,128)(2,1)S(1)}, bf16[768,768]{1,0:T(8,128)(2,1)S...) custom-call(s32[12]{0:T(128)S(1)} %copy-done.13, ...), custom_call_target="tpu_custom_call", output_to_operand_aliasing={{0}: (5, {}), {1}: (6, {}), {2}: (7, {}), {3}: (8, {}), {4}... | custom-call | tf_op jit(solution)/shard_map/attend1/pallas_call | solution.py:373
  78.0 3.3 %feed1.1 = (bf16[768,1536]{1,0:T(8,128)(2,1)S(1)}, bf16[768,1536]{1,0:T(8,128)(2,1)S(1)}, bf16[384,768]{1,0:T(8,128)(2,1)S(1)}, f32[1,6912]{1,0:T(1,128)S(1)}) custom-call(bf16[768,768]{1,0:T(8,128)(2,1)S(1)} %get-tuple-element.116.n2.refs_1_, f32[1,7680]{1,0:T(1,128)S(1)} %small.1, ...), custom_call_target="tpu_custom_call", output_to_operand_aliasing={{0}: (6, {}), {1}: (7, {})} | custom-call | tf_op jit(solution)/shard_map/feed1/pallas_call | solution.py:373
  81.3 1.6 collective-permute-start.26
  82.9 3.1 %grad_up.1 = (bf16[8,48,1536]{2,1,0:T(8,128)(2,1)S(1)}, bf16[8,48,1536]{2,1,0:T(8,128)(2,1)S(1)}) custom-call(s32[6]{0:T(128)S(1)} %stack.27.refs_0_.where.refs_3_, bf16[768,768]{1,0:T(8,128)(2,1)S(1)} %get-tuple-element.116.n2.refs_1_, bf16[768,1536]{1,0:T(8,128)(2,1)S(1)} %get-tuple-element.151.refs_2_), custom_call_target="tpu_custom_call" | custom-call | tf_op jit(solution)/shard_map/grad_up/pallas_call | solution.py:564
  86.0 2.0 %collective-permute-done.19.other = bf16[384,768]{1,0:T(8,128)(2,1)S(1)} collective-permute-done((bf16[384,768]{1,0:T(8,128)(2,1)S(1)}, bf16[384,768]{1,0:T(8,128)(2,1)S(1)}, u32[]{:S(2)}, u32[]{:S(2)}) %collective-permute-start.19) | collective-permute-done | bytes 589856 | tf_op jit(solution)/shard_map/ppermute | solution.py:466
  88.0 3.1 %grad_dn.1 = (bf16[8,48,1536]{2,1,0:T(8,128)(2,1)S(1)}, bf16[8,48,1536]{2,1,0:T(8,128)(2,1)S(1)}) custom-call(s32[6]{0:T(128)S(1)} %stack.27.refs_0_.where.refs_3_, bf16[768,768]{1,0:T(8,128)(2,1)S(1)} %bitcast.26, bf16[768,1536]{1,0:T(8,128)(2,1)S(1)} %get-tuple-element.123.refs_2_.act, bf16[8,48,1536]{2,1,0:T(8,128)(2,1)S(1)} %a_up.1.refs_1_.refs_3_), custom_call_target="tpu_custom_call" | custom-call | flops 16499999744 | tf_op jit(solution)/shard_map/grad_dn/pallas_call | solution.py:564
  94.8 7.9 %back0.1 = (bf16[768,768]{1,0:T(8,128)(2,1)S(1)}, bf16[768,2304]{1,0:T(8,128)(2,1)S(1)}, f32[1,6912]{1,0:T(1,128)S(1)}) custom-call(f32[768,768]{1,0:T(8,128)S(1)} %get-tuple-element.115.middle, bf16[384,768]{1,0:T(8,128)(2,1)S(1)} %get-tuple-element.126.own, bf16[384,768]{1,0:T(8,128)(2,1)S(1)} %collective-permute-done.19.other, ...), custom_call_target="tpu_custom_call" | custom-call | flops 16499999744 | tf_op jit(solution)/shard_map/back0/pallas_call | solution.py:373
  102.7 7.9 %back1.1 = (bf16[768,768]{1,0:T(8,128)(2,1)S(1)}, bf16[768,2304]{1,0:T(8,128)(2,1)S(1)}, f32[1,6912]{1,0:T(1,128)S(1)}) custom-call(f32[768,768]{1,0:T(8,128)S(1)} %get-tuple-element.115.middle, bf16[384,768]{1,0:T(8,128)(2,1)S(1)} %get-tuple-element.135.own, ...), custom_call_target="tpu_custom_call", output_to_operand_aliasing={{0}: (11, {}), {1}: (12, {})} | custom-call | flops 2200000000 | tf_op jit(solution)/shard_map/back1/pallas_call | solution.py:373
  110.6 2.0 %grad_out.1 = (bf16[8,48,384]{2,1,0:T(8,128)(2,1)S(1)}, bf16[8,48,384]{2,1,0:T(8,128)(2,1)S(1)}) custom-call(s32[6]{0:T(128)S(1)} %stack.27.refs_0_.where.refs_3_, bf16[768,768]{1,0:T(8,128)(2,1)S(1)} %get-tuple-element.157.refs_1_.gp, bf16[768,384]{1,0:T(8,128)(2,1)S(1)} %get-tuple-element.158.refs_2_), custom_call_target="tpu_custom_call" | custom-call | tf_op jit(solution)/shard_map/grad_out/pallas_call | solution.py:564
  113.7 1.6 collective-permute-start.32
  116.4 3.7 %rows0.1 = (bf16[768,768]{1,0:T(8,128)(2,1)}, f32[1,6912]{1,0:T(1,128)S(1)}) custom-call(s32[6]{0:T(128)S(1)} %stack.27.refs_0_.where.refs_3_, bf16[768,2304]{1,0:T(8,128)(2,1)S(1)} %get-tuple-element.144.refs_2_.gqkv, bf16[2,768,1536]{2,1,0:T(8,128)(2,1)S(1)} %get-tuple-element.106.refs_0_.w, bf16[768,768]{1,0:T(8,128)(2,1)S(1)} %bitcast.22, ...), custom_call_target="tpu_custom_call" | custom-call | tf_op jit(solution)/shard_map/rows0/pallas_call | solution.py:373
  120.0 3.7 %rows1.1 = (bf16[768,768]{1,0:T(8,128)(2,1)}, f32[1,6912]{1,0:T(1,128)S(1)}) custom-call(s32[6]{0:T(128)S(1)} %stack.27.refs_0_.where.refs_3_, bf16[768,2304]{1,0:T(8,128)(2,1)S(1)} %get-tuple-element.144.refs_2_.gqkv, bf16[2,768,1536]{2,1,0:T(8,128)(2,1)S(1)} %get-tuple-element.106.refs_0_.w, ...), custom_call_target="tpu_custom_call", output_to_operand_aliasing={{0}: (8, {})} | custom-call | tf_op jit(solution)/shard_map/rows1/pallas_call | solution.py:373
  123.7 2.8 %grad_qkv.1 = (bf16[8,48,1152]{2,1,0:T(8,128)(2,1)S(1)}, bf16[8,48,1152]{2,1,0:T(8,128)(2,1)S(1)}) custom-call(s32[6]{0:T(128)S(1)} %stack.27.refs_0_.where.refs_3_, bf16[768,768]{1,0:T(8,128)(2,1)S(1)} %get-tuple-element.134.refs_1_, bf16[768,2304]{1,0:T(8,128)(2,1)S(1)} %get-tuple-element.144.refs_2_.gqkv), custom_call_target="tpu_custom_call" | custom-call | flops 2200000000 | tf_op jit(solution)/shard_map/grad_qkv/pallas_call | solution.py:564
  131.7 2.8 %collective-permute-done.35.refs_2_ = bf16[240,384]{1,0:T(8,128)(2,1)S(1)} collective-permute-done((bf16[240,384]{1,0:T(8,128)(2,1)S(1)}, bf16[240,384]{1,0:T(8,128)(2,1)S(1)}, u32[]{:S(2)}, u32[]{:S(2)}) %collective-permute-start.35) | collective-permute-done | bytes 184352 | tf_op jit(solution)/shard_map/ppermute | solution.py:466
  135.2 3.9 %collective-permute-start.36 = (bf16[144,384]{1,0:T(8,128)(2,1)S(1)}, bf16[144,384]{1,0:T(8,128)(2,1)S(1)}, u32[]{:S(2)}, u32[]{:S(2)}) collective-permute-start(bf16[144,384]{1,0:T(8,128)(2,1)S(1)} %get-tuple-element.175), channel_id=1, source_target_pairs={{0,16},{2,18},{4,20},{6,22},{8,24},{10,26},{12,28},{14,30},{16,0},... | collective-permute-start | bytes 331784 | tf_op jit(solution)/shard_map/ppermute | solution.py:466
  144.0 2.0 %collective-permute-start.39 = (bf16[48,1536]{1,0:T(8,128)(2,1)S(1)}, bf16[48,1536]{1,0:T(8,128)(2,1)S(1)}, u32[]{:S(2)}, u32[]{:S(2)}) collective-permute-start(bf16[48,1536]{1,0:T(8,128)(2,1)S(1)} %get-tuple-element.189.refs_3_), channel_id=1, source_target_pairs={{0,16},{2,18},{4,20},{6,22},{8,24},{10,26},{12,28},{14,30},{16,0},... | collective-permute-start | bytes 442376 | tf_op jit(solution)/shard_map/ppermute | solution.py:466
  149.2 3.1 %collective-permute-done.24.refs_2_ = bf16[2,48,1536]{2,1,0:T(8,128)(2,1)S(1)} collective-permute-done((bf16[2,48,1536]{2,1,0:T(8,128)(2,1)S(1)}, bf16[2,48,1536]{2,1,0:T(8,128)(2,1)S(1)}, u32[]{:S(2)}, u32[]{:S(2)}) %collective-permute-start.24) | collective-permute-done | bytes 294944 | tf_op jit(solution)/shard_map/ppermute | solution.py:466
  155.0 4.1 %collective-permute-done.29.refs_2_ = bf16[2,48,1152]{2,1,0:T(8,128)(2,1)S(1)} collective-permute-done((bf16[2,48,1152]{2,1,0:T(8,128)(2,1)S(1)}, bf16[2,48,1152]{2,1,0:T(8,128)(2,1)S(1)}, u32[]{:S(2)}, u32[]{:S(2)}) %collective-permute-start.29) | collective-permute-done | bytes 221216 | tf_op jit(solution)/shard_map/ppermute | solution.py:466
  (119 shorter events, 48.3 us)
Async XLA Ops:
  0.7 7.2 %collective-permute-start = (f32[2,384]{1,0:T(2,128)}, f32[2,384]{1,0:T(2,128)S(1)}, u32[]{:S(2)}, u32[]{:S(2)}) collective-permute-start(f32[2,384]{1,0:T(2,128)} %refs_1_.2), channel_id=1, source_target_pairs={{0,1},{1,0},{2,3},{3,2},{4,5},{5,4},{6,7},{7,6},{8,9},{9,8},{10,11... | collective-permute-start | bytes 9224 | tf_op jit(solution)/shard_map/ppermute | solution.py:466
  3.7 17.1 %collective-permute-start.7 = (bf16[48,1536]{1,0:T(8,128)(2,1)}, bf16[48,1536]{1,0:T(8,128)(2,1)S(1)}, u32[]{:S(2)}, u32[]{:S(2)}) collective-permute-start(bf16[48,1536]{1,0:T(8,128)(2,1)} %refs_1_.3), channel_id=1, source_target_pairs={{0,16},{2,18},{4,20},{6,22},{8,24},{10,26},{12,28},{14,30},{16,0},... | collective-permute-start | bytes 442376 | tf_op jit(solution)/shard_map/ppermute | solution.py:466
  7.9 16.0 %collective-permute-start.1 = (bf16[48,1536]{1,0:T(8,128)(2,1)S(1)}, bf16[48,1536]{1,0:T(8,128)(2,1)S(1)}, u32[]{:S(2)}, u32[]{:S(2)}) collective-permute-start(bf16[48,1536]{1,0:T(8,128)(2,1)S(1)} %pad_maximum_fusion.refs_1_), channel_id=1, source_target_pairs={{0,16},{2,18},{4,20},{6,22},{8,24},{10,26},{12,28},{14,30},{16,0},... | collective-permute-start | bytes 442376 | tf_op jit(solution)/shard_map/ppermute | solution.py:466
  8.6 17.4 %collective-permute-start.11 = (bf16[48,1536]{1,0:T(8,128)(2,1)}, bf16[48,1536]{1,0:T(8,128)(2,1)S(1)}, u32[]{:S(2)}, u32[]{:S(2)}) collective-permute-start(bf16[48,1536]{1,0:T(8,128)(2,1)} %bitcast.32), channel_id=1, source_target_pairs={{0,16},{2,18},{4,20},{6,22},{8,24},{10,26},{12,28},{14,30},{16,0},... | collective-permute-start | bytes 442376 | tf_op jit(solution)/shard_map/ppermute | solution.py:466
  22.2 6.8 %collective-permute-start.15 = (bf16[2,48,1536]{2,1,0:T(8,128)(2,1)S(1)}, bf16[2,48,1536]{2,1,0:T(8,128)(2,1)S(1)}, u32[]{:S(2)}, u32[]{:S(2)}) collective-permute-start(bf16[2,48,1536]{2,1,0:T(8,128)(2,1)S(1)} %p_up.1.refs_1_), channel_id=1, source_target_pairs={{0,4},{2,6},{4,0},{6,2},{8,12},{10,14},{12,8},{14,10},{16,20},{18,... | collective-permute-start | bytes 884744 | tf_op jit(solution)/shard_map/ppermute | solution.py:466
  24.5 10.0 %collective-permute-start.2 = (bf16[2,48,1536]{2,1,0:T(8,128)(2,1)S(1)}, bf16[2,48,1536]{2,1,0:T(8,128)(2,1)S(1)}, u32[]{:S(2)}, u32[]{:S(2)}) collective-permute-start(bf16[2,48,1536]{2,1,0:T(8,128)(2,1)S(1)} %p_att.1.refs_1_), channel_id=1, source_target_pairs={{0,8},{2,10},{4,12},{6,14},{8,0},{10,2},{12,4},{14,6},{16,24},{18,... | collective-permute-start | bytes 884744 | tf_op jit(solution)/shard_map/ppermute | solution.py:466
  26.6 12.0 %collective-permute-start.12 = (bf16[2,48,1536]{2,1,0:T(8,128)(2,1)S(1)}, bf16[2,48,1536]{2,1,0:T(8,128)(2,1)S(1)}, u32[]{:S(2)}, u32[]{:S(2)}) collective-permute-start(bf16[2,48,1536]{2,1,0:T(8,128)(2,1)S(1)} %p_dn.1.refs_1_), channel_id=1, source_target_pairs={{0,8},{2,10},{4,12},{6,14},{8,0},{10,2},{12,4},{14,6},{16,24},{18,... | collective-permute-start | bytes 884744 | tf_op jit(solution)/shard_map/ppermute | solution.py:466
  35.1 13.6 %collective-permute-start.3 = (bf16[4,48,1536]{2,1,0:T(8,128)(2,1)S(1)}, bf16[4,48,1536]{2,1,0:T(8,128)(2,1)S(1)}, u32[]{:S(2)}, u32[]{:S(2)}) collective-permute-start(bf16[4,48,1536]{2,1,0:T(8,128)(2,1)S(1)} %a_att.1.refs_0_), channel_id=1, source_target_pairs={{0,4},{2,6},{4,0},{6,2},{8,12},{10,14},{12,8},{14,10},{16,20},{18,... | collective-permute-start | bytes 1769480 | tf_op jit(solution)/shard_map/ppermute | solution.py:466
  36.6 13.2 %collective-permute-start.6 = (bf16[4,48,1536]{2,1,0:T(8,128)(2,1)S(1)}, bf16[4,48,1536]{2,1,0:T(8,128)(2,1)S(1)}, u32[]{:S(2)}, u32[]{:S(2)}) collective-permute-start(bf16[4,48,1536]{2,1,0:T(8,128)(2,1)S(1)} %a_att.1.refs_0_), channel_id=1, source_target_pairs={{0,1},{1,0},{2,3},{3,2},{4,5},{5,4},{6,7},{7,6},{8,9},{9,8},{10,11... | collective-permute-start | bytes 1769480 | tf_op jit(solution)/shard_map/ppermute | solution.py:466
  39.3 13.1 %collective-permute-start.16 = (bf16[4,48,1536]{2,1,0:T(8,128)(2,1)S(1)}, bf16[4,48,1536]{2,1,0:T(8,128)(2,1)S(1)}, u32[]{:S(2)}, u32[]{:S(2)}) collective-permute-start(bf16[4,48,1536]{2,1,0:T(8,128)(2,1)S(1)} %px_up.1.refs_1_), channel_id=1, source_target_pairs={{0,8},{2,10},{4,12},{6,14},{8,0},{10,2},{12,4},{14,6},{16,24},{18,... | collective-permute-start | bytes 1769480 | tf_op jit(solution)/shard_map/ppermute | solution.py:466
  40.1 13.0 %collective-permute-start.4 = (bf16[4,48,1536]{2,1,0:T(8,128)(2,1)S(1)}, bf16[4,48,1536]{2,1,0:T(8,128)(2,1)S(1)}, u32[]{:S(2)}, u32[]{:S(2)}) collective-permute-start(bf16[4,48,1536]{2,1,0:T(8,128)(2,1)S(1)} %a_att.1.refs_0_), channel_id=1, source_target_pairs={{0,2},{2,0},{4,6},{6,4},{8,10},{10,8},{12,14},{14,12},{16,18},{18,... | collective-permute-start | bytes 1769480 | tf_op jit(solution)/shard_map/ppermute | solution.py:466
  40.1 18.5 %collective-permute-start.13 = (bf16[4,48,1536]{2,1,0:T(8,128)(2,1)S(1)}, bf16[4,48,1536]{2,1,0:T(8,128)(2,1)S(1)}, u32[]{:S(2)}, u32[]{:S(2)}) collective-permute-start(bf16[4,48,1536]{2,1,0:T(8,128)(2,1)S(1)} %a_dn.1.refs_4_), channel_id=1, source_target_pairs={{0,4},{2,6},{4,0},{6,2},{8,12},{10,14},{12,8},{14,10},{16,20},{18,... | collective-permute-start | bytes 1769480 | tf_op jit(solution)/shard_map/ppermute | solution.py:466
  48.7 11.1 %collective-permute-start.8 = (bf16[4,48,1536]{2,1,0:T(8,128)(2,1)S(1)}, bf16[4,48,1536]{2,1,0:T(8,128)(2,1)S(1)}, u32[]{:S(2)}, u32[]{:S(2)}) collective-permute-start(bf16[4,48,1536]{2,1,0:T(8,128)(2,1)S(1)} %collective-permute-done.3.refs_1_), channel_id=1, source_target_pairs={{0,1},{1,0},{2,3},{3,2},{4,5},{5,4},{6,7},{7,6},{8,9},{9,8},{10,11... | collective-permute-start | bytes 1769480 | tf_op jit(solution)/shard_map/ppermute | solution.py:466
  49.9 9.9 %collective-permute-start.9 = (bf16[4,48,1536]{2,1,0:T(8,128)(2,1)S(1)}, bf16[4,48,1536]{2,1,0:T(8,128)(2,1)S(1)}, u32[]{:S(2)}, u32[]{:S(2)}) collective-permute-start(bf16[4,48,1536]{2,1,0:T(8,128)(2,1)S(1)} %collective-permute-done.6.refs_4_), channel_id=1, source_target_pairs={{0,2},{2,0},{4,6},{6,4},{8,10},{10,8},{12,14},{14,12},{16,18},{18,... | collective-permute-start | bytes 1769480 | tf_op jit(solution)/shard_map/ppermute | solution.py:466
  53.0 14.6 %collective-permute-start.17 = (bf16[8,48,1536]{2,1,0:T(8,128)(2,1)S(1)}, bf16[8,48,1536]{2,1,0:T(8,128)(2,1)S(1)}, u32[]{:S(2)}, u32[]{:S(2)}) collective-permute-start(bf16[8,48,1536]{2,1,0:T(8,128)(2,1)S(1)} %a_up.1.refs_1_.refs_3_), channel_id=1, source_target_pairs={{0,2},{2,0},{4,6},{6,4},{8,10},{10,8},{12,14},{14,12},{16,18},{18,... | collective-permute-start | bytes 3538952 | tf_op jit(solution)/shard_map/ppermute | solution.py:466
  53.1 7.8 %collective-permute-start.5 = (bf16[4,48,1536]{2,1,0:T(8,128)(2,1)S(1)}, bf16[4,48,1536]{2,1,0:T(8,128)(2,1)S(1)}, u32[]{:S(2)}, u32[]{:S(2)}) collective-permute-start(bf16[4,48,1536]{2,1,0:T(8,128)(2,1)S(1)} %collective-permute-done.3.refs_1_), channel_id=1, source_target_pairs={{0,2},{2,0},{4,6},{6,4},{8,10},{10,8},{12,14},{14,12},{16,18},{18,... | collective-permute-start | bytes 1769480 | tf_op jit(solution)/shard_map/ppermute | solution.py:466
  59.8 7.8 %collective-permute-start.18 = (bf16[4,48,1536]{2,1,0:T(8,128)(2,1)S(1)}, bf16[4,48,1536]{2,1,0:T(8,128)(2,1)S(1)}, u32[]{:S(2)}, u32[]{:S(2)}) collective-permute-start(bf16[4,48,1536]{2,1,0:T(8,128)(2,1)S(1)} %a_dn.1.refs_4_), channel_id=1, source_target_pairs={{0,2},{2,0},{4,6},{6,4},{8,10},{10,8},{12,14},{14,12},{16,18},{18,... | collective-permute-start | bytes 1769480 | tf_op jit(solution)/shard_map/ppermute | solution.py:466
  71.8 16.2 %collective-permute-start.19 = (bf16[384,768]{1,0:T(8,128)(2,1)S(1)}, bf16[384,768]{1,0:T(8,128)(2,1)S(1)}, u32[]{:S(2)}, u32[]{:S(2)}) collective-permute-start(bf16[384,768]{1,0:T(8,128)(2,1)S(1)} %get-tuple-element.126.own), channel_id=1, source_target_pairs={{0,1},{1,0},{2,3},{3,2},{4,5},{5,4},{6,7},{7,6},{8,9},{9,8},{10,11... | collective-permute-start | bytes 1769480 | tf_op jit(solution)/shard_map/ppermute | solution.py:466
  81.3 21.4 %collective-permute-start.26 = (bf16[384,768]{1,0:T(8,128)(2,1)S(1)}, bf16[384,768]{1,0:T(8,128)(2,1)S(1)}, u32[]{:S(2)}, u32[]{:S(2)}) collective-permute-start(bf16[384,768]{1,0:T(8,128)(2,1)S(1)} %get-tuple-element.135.own), channel_id=1, source_target_pairs={{0,1},{1,0},{2,3},{3,2},{4,5},{5,4},{6,7},{7,6},{8,9},{9,8},{10,11... | collective-permute-start | bytes 1769480 | tf_op jit(solution)/shard_map/ppermute | solution.py:466
  92.4 20.7 %collective-permute-start.31 = (bf16[4,48,1536]{2,1,0:T(8,128)(2,1)S(1)}, bf16[4,48,1536]{2,1,0:T(8,128)(2,1)S(1)}, u32[]{:S(2)}, u32[]{:S(2)}) collective-permute-start(bf16[4,48,1536]{2,1,0:T(8,128)(2,1)S(1)} %get-tuple-element.156), channel_id=1, source_target_pairs={{0,4},{2,6},{4,0},{6,2},{8,12},{10,14},{12,8},{14,10},{16,20},{18,... | collective-permute-start | bytes 1769480 | tf_op jit(solution)/shard_map/ppermute | solution.py:466
  112.6 14.4 %collective-permute-start.33 = (bf16[8,48,384]{2,1,0:T(8,128)(2,1)S(1)}, bf16[8,48,384]{2,1,0:T(8,128)(2,1)S(1)}, u32[]{:S(2)}, u32[]{:S(2)}) collective-permute-start(bf16[8,48,384]{2,1,0:T(8,128)(2,1)S(1)} %get-tuple-element.169.refs_3_), channel_id=1, source_target_pairs={{0,2},{2,0},{4,6},{6,4},{8,10},{10,8},{12,14},{14,12},{16,18},{18,... | collective-permute-start | bytes 884744 | tf_op jit(solution)/shard_map/ppermute | solution.py:466
  113.7 13.4 %collective-permute-start.32 = (bf16[2,48,1536]{2,1,0:T(8,128)(2,1)S(1)}, bf16[2,48,1536]{2,1,0:T(8,128)(2,1)S(1)}, u32[]{:S(2)}, u32[]{:S(2)}) collective-permute-start(bf16[2,48,1536]{2,1,0:T(8,128)(2,1)S(1)} %get-tuple-element.161), channel_id=1, source_target_pairs={{0,8},{2,10},{4,12},{6,14},{8,0},{10,2},{12,4},{14,6},{16,24},{18,... | collective-permute-start | bytes 884744 | tf_op jit(solution)/shard_map/ppermute | solution.py:466
  115.2 23.9 %collective-permute-start.21 = (bf16[4,48,1536]{2,1,0:T(8,128)(2,1)S(1)}, bf16[4,48,1536]{2,1,0:T(8,128)(2,1)S(1)}, u32[]{:S(2)}, u32[]{:S(2)}) collective-permute-start(bf16[4,48,1536]{2,1,0:T(8,128)(2,1)S(1)} %get-tuple-element.128.refs_0_), channel_id=1, source_target_pairs={{0,4},{2,6},{4,0},{6,2},{8,12},{10,14},{12,8},{14,10},{16,20},{18,... | collective-permute-start | bytes 1769480 | tf_op jit(solution)/shard_map/ppermute | solution.py:466
  129.5 18.8 %collective-permute-start.23 = (bf16[384,768]{1,0:T(8,128)(2,1)S(1)}, bf16[384,768]{1,0:T(8,128)(2,1)S(1)}, u32[]{:S(2)}, u32[]{:S(2)}) collective-permute-start(bf16[384,768]{1,0:T(8,128)(2,1)S(1)} %down0.1.own), channel_id=1, source_target_pairs={{0,1},{1,0},{2,3},{3,2},{4,5},{5,4},{6,7},{7,6},{8,9},{9,8},{10,11... | collective-permute-start | bytes 1769480 | tf_op jit(solution)/shard_map/ppermute | solution.py:466
  130.8 16.0 %collective-permute-start.28 = (bf16[4,48,1152]{2,1,0:T(8,128)(2,1)S(1)}, bf16[4,48,1152]{2,1,0:T(8,128)(2,1)S(1)}, u32[]{:S(2)}, u32[]{:S(2)}) collective-permute-start(bf16[4,48,1152]{2,1,0:T(8,128)(2,1)S(1)} %get-tuple-element.148), channel_id=1, source_target_pairs={{0,4},{2,6},{4,0},{6,2},{8,12},{10,14},{12,8},{14,10},{16,20},{18,... | collective-permute-start | bytes 1327112 | tf_op jit(solution)/shard_map/ppermute | solution.py:466
  135.2 8.8 %collective-permute-start.36 = (bf16[144,384]{1,0:T(8,128)(2,1)S(1)}, bf16[144,384]{1,0:T(8,128)(2,1)S(1)}, u32[]{:S(2)}, u32[]{:S(2)}) collective-permute-start(bf16[144,384]{1,0:T(8,128)(2,1)S(1)} %get-tuple-element.175), channel_id=1, source_target_pairs={{0,16},{2,18},{4,20},{6,22},{8,24},{10,26},{12,28},{14,30},{16,0},... | collective-permute-start | bytes 331784 | tf_op jit(solution)/shard_map/ppermute | solution.py:466
  139.7 12.6 %collective-permute-start.24 = (bf16[2,48,1536]{2,1,0:T(8,128)(2,1)S(1)}, bf16[2,48,1536]{2,1,0:T(8,128)(2,1)S(1)}, u32[]{:S(2)}, u32[]{:S(2)}) collective-permute-start(bf16[2,48,1536]{2,1,0:T(8,128)(2,1)S(1)} %get-tuple-element.131), channel_id=1, source_target_pairs={{0,8},{2,10},{4,12},{6,14},{8,0},{10,2},{12,4},{14,6},{16,24},{18,... | collective-permute-start | bytes 884744 | tf_op jit(solution)/shard_map/ppermute | solution.py:466
  141.5 22.1 %collective-permute-start.22 = (bf16[384,768]{1,0:T(8,128)(2,1)S(1)}, bf16[384,768]{1,0:T(8,128)(2,1)S(1)}, u32[]{:S(2)}, u32[]{:S(2)}) collective-permute-start(bf16[384,768]{1,0:T(8,128)(2,1)S(1)} %down1.1.own), channel_id=1, source_target_pairs={{0,1},{1,0},{2,3},{3,2},{4,5},{5,4},{6,7},{7,6},{8,9},{9,8},{10,11... | collective-permute-start | bytes 1769480 | tf_op jit(solution)/shard_map/ppermute | solution.py:466
  144.0 9.6 %collective-permute-start.39 = (bf16[48,1536]{1,0:T(8,128)(2,1)S(1)}, bf16[48,1536]{1,0:T(8,128)(2,1)S(1)}, u32[]{:S(2)}, u32[]{:S(2)}) collective-permute-start(bf16[48,1536]{1,0:T(8,128)(2,1)S(1)} %get-tuple-element.189.refs_3_), channel_id=1, source_target_pairs={{0,16},{2,18},{4,20},{6,22},{8,24},{10,26},{12,28},{14,30},{16,0},... | collective-permute-start | bytes 442376 | tf_op jit(solution)/shard_map/ppermute | solution.py:466
  146.8 7.6 %collective-permute-start.37 = (bf16[96,384]{1,0:T(8,128)(2,1)S(1)}, bf16[96,384]{1,0:T(8,128)(2,1)S(1)}, u32[]{:S(2)}, u32[]{:S(2)}) collective-permute-start(bf16[96,384]{1,0:T(8,128)(2,1)S(1)} %get-tuple-element.178), channel_id=1, source_target_pairs={{0,4},{2,6},{4,0},{6,2},{8,12},{10,14},{12,8},{14,10},{16,20},{18,... | collective-permute-start | bytes 221192 | tf_op jit(solution)/shard_map/ppermute | solution.py:466
  148.3 10.8 %collective-permute-start.29 = (bf16[2,48,1152]{2,1,0:T(8,128)(2,1)S(1)}, bf16[2,48,1152]{2,1,0:T(8,128)(2,1)S(1)}, u32[]{:S(2)}, u32[]{:S(2)}) collective-permute-start(bf16[2,48,1152]{2,1,0:T(8,128)(2,1)S(1)} %get-tuple-element.150), channel_id=1, source_target_pairs={{0,8},{2,10},{4,12},{6,14},{8,0},{10,2},{12,4},{14,6},{16,24},{18,... | collective-permute-start | bytes 663560 | tf_op jit(solution)/shard_map/ppermute | solution.py:466
  152.9 7.9 %collective-permute-start.25 = (bf16[48,1536]{1,0:T(8,128)(2,1)S(1)}, bf16[48,1536]{1,0:T(8,128)(2,1)S(1)}, u32[]{:S(2)}, u32[]{:S(2)}) collective-permute-start(bf16[48,1536]{1,0:T(8,128)(2,1)S(1)} %get-tuple-element.133), channel_id=1, source_target_pairs={{0,16},{2,18},{4,20},{6,22},{8,24},{10,26},{12,28},{14,30},{16,0},... | collective-permute-start | bytes 442376 | tf_op jit(solution)/shard_map/ppermute | solution.py:466
  (22 other events, 278.5 us)
